TPU v7x, 32 devices: a whole 2x2x4 slice. The times are simulated.
32 devices in a mesh: freq: 8 (over z, x), src: 2 (over y), rcv: 2 (over core).
Axes of the slice: x: 2, y: 2, z: 4, core: 2. Of those that a mesh axis runs over, the one named last changes fastest.
Arguments:
- traces: float32 [1024, 1024, 256], P(('src', 'freq'), 'rcv'), may hold values from -6 to 6
Outputs:
- multiples: float32 [2, 24, 1024, 1024], P(None, 'freq', 'src', 'rcv')
All inputs are finite; a program needn't handle non-finite values.
Results may differ from a plain program's by a relative error of at most 0.000098.
Values sent between devices are 32-bit elements; how exact they have to be, the bound alone decides.
No kernel may reach another device: no remote copies, remote signals or barrier semaphores. Data moves between devices by JAX's collectives and lax.ppermute only.
A program may use at most 128 MiB of HBM per device.

v0:
```python
import math

import jax
import jax.numpy as jnp
from jax import lax
from jax.sharding import PartitionSpec as P

N = 1024
FPD = 3


def dft_matrix(n_time, n_freq):
    times = jnp.arange(n_time, dtype=jnp.int32)
    bins = jnp.arange(n_freq, dtype=jnp.int32)
    phase = times[:, None] * bins[None, :] % n_time
    angle = phase.astype(jnp.float32) * (2.0 * math.pi / n_time)
    both = jnp.stack([jnp.cos(angle), -jnp.sin(angle)], axis=-1)
    return both.reshape(n_time, 2 * n_freq) * (1.0 / math.sqrt(n_time))


def batched_dot(left, right):
    return jnp.einsum(
        "mgq,mqn->mgn",
        left,
        right,
        precision=lax.Precision.HIGHEST,
        preferred_element_type=jnp.float32,
    )


def complex_product(left_re, left_im, right_re, right_im):
    real_part = batched_dot(left_re, right_re) - batched_dot(left_im, right_im)
    imag_part = batched_dot(left_re, right_im) + batched_dot(left_im, right_re)
    return (real_part, imag_part)


def per_device(traces):
    n_time = traces.shape[2]
    n_freq = FPD * lax.axis_size("freq")
    dft_table = dft_matrix(n_time, n_freq)
    spectra = jnp.einsum(
        "srt,tk->ksr",
        traces,
        dft_table,
        precision=lax.Precision.HIGHEST,
        preferred_element_type=jnp.float32,
    )
    regrouped = lax.all_to_all(spectra, "freq", split_axis=0, concat_axis=1, tiled=True)
    src_rows = regrouped.shape[1]
    rcv_cols = regrouped.shape[2]
    split_parts = regrouped.reshape(FPD, 2, src_rows, rcv_cols)
    local_re = split_parts[:, 0]
    local_im = split_parts[:, 1]
    col_re, col_im = (
        lax.all_gather(local_re, "src", axis=1, tiled=True),
        lax.all_gather(local_im, "src", axis=1, tiled=True),
    )
    piece_re = lax.all_gather(local_re, "rcv", axis=2, tiled=True)
    piece_im = lax.all_gather(local_im, "rcv", axis=2, tiled=True)
    real_part, imag_part = complex_product(piece_re, piece_im, col_re, col_im)
    scale = -1.0 / math.sqrt(N)
    return jnp.stack([real_part, imag_part]) * scale


def solution(mesh):
    in_specs = (P(("src", "freq"), "rcv", None),)
    out_specs = P(None, "freq", "src", "rcv")
    return jax.shard_map(
        per_device, mesh=mesh, in_specs=in_specs, out_specs=out_specs, check_vma=False
    )
```

profile of v0, /device:TPU:0, one launch (start us, length us, event | category | flops | bytes accessed | tf_op | source)
XLA Modules:
  0.0 441.3 jit_solution(5281717539840629216)
XLA Ops:
  6.5 0.0 all-gather.15.cloned.1.call-start
  6.5 0.1 sine_negate_fusion
  6.7 40.8 %fusion.27 = f32[48,64,512]{2,0,1:T(8,128)} fusion(f32[256,48,1]{0,1,2:T(8,128)S(1)} %reshape.83, f32[64,512,256]{2,1,0:T(8,128)} %param.1), kind=kOutput, calls=%fused_computation.29 | convolution fusion | flops 4831838208 | bytes 39895040 | tf_op jit(solution)/shard_map/srt,tk->ksr/dot_general | solution.py:41
  47.5 6.4 %copy.15 = f32[48,64,512]{2,1,0:T(8,128)S(1)} copy(f32[48,64,512]{2,0,1:T(8,128)} %fusion.27) | data formatting | bytes 12582912 | tf_op jit(solution)/shard_map/srt,tk->ksr/dot_general | solution.py:41
  53.9 145.2 %all_to_all.15 = f32[48,64,512]{2,1,0:T(8,128)S(1)} all-to-all(f32[48,64,512]{2,1,0:T(8,128)S(1)} %copy.15), channel_id=1, replica_groups=mesh['freq'=8,'src'=2,'rcv'=2] {'freq'}, dimensions={0} | all-to-all | bytes 12582912 | tf_op jit(solution)/shard_map/all_to_all | solution.py:48
  199.1 1.2 copy.16
  200.4 3.5 slice_bitcast_fusion.1
  203.8 0.0 all-gather.15.cloned.1.call-update
  203.8 0.0 all-gather.13.cloned.1.call-start
  203.9 0.7 all-gather.13.cloned.1.call-update
  204.6 0.0 all-gather.9.cloned.1.call-start
  204.6 0.7 all-gather.9.cloned.1.call-update
  205.3 0.2 all-gather.11.cloned.1.call-start
  205.6 0.3 all-gather.11.cloned.1.call-update
  205.9 77.5 %all-gather.15.cloned.1.call-done = f32[3,1,1024,512]{3,2,0,1:T(8,128)} async-done(((f32[3,1,512,512]{3,2,0,1:T(8,128)}), f32[3,1,1024,512]{3,2,0,1:T(8,128)}) %all-gather.15.cloned.1.call-update) | async-done | bytes 6291472 | tf_op jit(solution)/shard_map/all_gather | solution.py:56
  283.4 18.3 %all-gather.13.cloned.1.call-done = f32[3,1,512,1024]{3,2,0,1:T(8,128)} async-done(((f32[3,1,512,512]{3,2,0,1:T(8,128)}), f32[3,1,512,1024]{3,2,0,1:T(8,128)}) %all-gather.13.cloned.1.call-update) | async-done | bytes 6291472 | tf_op jit(solution)/shard_map/all_gather | solution.py:59
  301.8 12.8 %fusion.2 = f32[3,512,512]{2,1,0:T(8,128)S(1)} fusion(f32[3,1,1024,512]{3,2,0,1:T(8,128)} %all-gather.15.cloned.1.call-done, f32[3,1,512,1024]{3,2,0,1:T(8,128)} %all-gather.13.cloned.1.call-done), kind=kOutput, calls=%fused_computation.3 | convolution fusion | flops 9663676416 | bytes 15728640 | tf_op jit(solution)/shard_map/mgq,mqn->mgn/dot_general | solution.py:22
  314.5 6.7 %all-gather.9.cloned.1.call-done = f32[3,1,512,1024]{3,2,0,1:T(8,128)} async-done(((f32[3,1,512,512]{3,2,0,1:T(8,128)}), f32[3,1,512,1024]{3,2,0,1:T(8,128)}) %all-gather.9.cloned.1.call-update) | async-done | bytes 6291472 | tf_op jit(solution)/shard_map/all_gather | solution.py:58
  321.3 16.8 %fusion = f32[3,512,512]{2,1,0:T(8,128)} fusion(f32[3,1,1024,512]{3,2,0,1:T(8,128)} %all-gather.15.cloned.1.call-done, f32[3,1,512,1024]{3,2,0,1:T(8,128)} %all-gather.9.cloned.1.call-done), kind=kOutput, calls=%fused_computation.1 | convolution fusion | flops 9663676416 | bytes 15728640 | tf_op jit(solution)/shard_map/mgq,mqn->mgn/dot_general | solution.py:22
  338.0 66.2 %all-gather.11.cloned.1.call-done = f32[3,1,1024,512]{3,2,0,1:T(8,128)} async-done(((f32[3,1,512,512]{3,2,0,1:T(8,128)}), f32[3,1,1024,512]{3,2,0,1:T(8,128)}) %all-gather.11.cloned.1.call-update) | async-done | bytes 6291472 | tf_op jit(solution)/shard_map/all_gather | solution.py:55
  404.3 13.7 %subtract_bitcast_fusion = f32[1,3,512,512]{3,2,1,0:T(8,128)S(1)} fusion(f32[3,512,512]{2,1,0:T(8,128)S(1)} %fusion.2, f32[3,1,1024,512]{3,2,0,1:T(8,128)} %all-gather.11.cloned.1.call-done, f32[3,1,512,1024]{3,2,0,1:T(8,128)} %all-gather.9.cloned.1.call-done), kind=kOutput, calls=%fused_computation.16 | convolution fusion | flops 9664462848 | bytes 18874368 | tf_op jit(solution)/shard_map/mgq,mqn->mgn/dot_general | solution.py:22
  417.9 0.0 copy-done
  418.0 13.4 %add_bitcast_fusion = f32[1,3,512,512]{3,2,1,0:T(8,128)S(1)} fusion(f32[3,512,512]{2,1,0:T(8,128)S(1)} %copy-done.1, f32[3,1,1024,512]{3,2,0,1:T(8,128)S(1)} %copy-done, f32[3,1,512,1024]{3,2,0,1:T(8,128)} %all-gather.13.cloned.1.call-done), kind=kOutput, calls=%fused_computation.15 | convolution fusion | flops 9664462848 | bytes 18874368 | tf_op jit(solution)/shard_map/mgq,mqn->mgn/dot_general | solution.py:22
  431.3 3.5 maximum_multiply_fusion
  (6 shorter events, 0.1 us)
Async XLA Ops:
  6.5 276.9 %all-gather.15.cloned.1.call-start = ((), (), s32[]{:S(2)}) async-start(), calls=%async_computation.4 | async-start | bytes 9437184 | tf_op jit(solution)/shard_map/all_gather | solution.py:56
  203.8 97.9 %all-gather.13.cloned.1.call-start = ((), (), s32[]{:S(2)}) async-start(), calls=%async_computation.3 | async-start | bytes 9437184 | tf_op jit(solution)/shard_map/all_gather | solution.py:59
  204.6 116.7 %all-gather.9.cloned.1.call-start = ((), (), s32[]{:S(2)}) async-start(), calls=%async_computation.1 | async-start | bytes 9437184 | tf_op jit(solution)/shard_map/all_gather | solution.py:58
  205.3 198.9 %all-gather.11.cloned.1.call-start = ((), (), s32[]{:S(2)}) async-start(), calls=%async_computation.2 | async-start | bytes 9437184 | tf_op jit(solution)/shard_map/all_gather | solution.py:55
  404.3 13.7 %copy-start = (f32[3,1,1024,512]{3,2,0,1:T(8,128)S(1)}, f32[3,1,1024,512]{3,2,0,1:T(8,128)}, u32[]{:S(2)}) copy-start(f32[3,1,1024,512]{3,2,0,1:T(8,128)} %all-gather.11.cloned.1.call-done) | copy-start | bytes 18874372
  404.3 13.7 %copy-start.1 = (f32[3,512,512]{2,1,0:T(8,128)S(1)}, f32[3,512,512]{2,1,0:T(8,128)}, u32[]{:S(2)}) copy-start(f32[3,512,512]{2,1,0:T(8,128)} %fusion) | copy-start | bytes 9437188
Sparse Core Ops, SparseCore 0:
  204.0 79.4 all-gather.14
  285.0 16.7 all-gather.12
  303.3 17.9 all-gather.8
  322.7 81.5 all-gather.10
where the time goes:
time: 442 us; the launch traced here: 441 us
  waiting for transfers between devices  171 us (39%)
  blocking collectives  145 us (33%)
  matrix products  97.3 us (22%)
  between operations  13.2 us (3%)
  local copies, waits for them, and re-layouts  11.2 us (3%)
    all_to_all x1, blocking collectives, per_device(): lax.all_to_all(spectra, 'freq', split_axis=0, concat_axis=1, tiled=True)  145 us
    all_gather x1, waiting for transfers between devices, per_device(): lax.all_gather(local_im, 'src', axis=1, tiled=True)  77.5 us
    all_gather x1, waiting for transfers between devices, per_device(): lax.all_gather(local_re, 'src', axis=1, tiled=True)  66.2 us
    dot_general x4, matrix products, batched_dot(): jnp.einsum('mgq,mqn->mgn', left, right, precision=lax.Precision.HIGHEST,...  56.6 us
    dot_general x1, matrix products, per_device(): jnp.einsum('srt,tk->ksr', traces, dft_table, precision=lax.Precision.HIGH...  40.8 us
    all_gather x1, waiting for transfers between devices, per_device(): piece_im = lax.all_gather(local_im, 'rcv', axis=2, tiled=True)  18.3 us
  transfers between devices with their start and end apart: 4, of which 4 were waited for; matrix products, arithmetic and copies ran while one was open for 7% of the time, Pallas kernels for 0%

commit v1 on v0

v1 whole, which is shorter than its diff:
```python
import functools
import math

import jax
import jax.numpy as jnp
from jax import lax
from jax.experimental import pallas as pl
from jax.experimental.pallas import tpu as pltpu
from jax.sharding import PartitionSpec as P

FPD = 3
WINDOW = 5
BF16 = jnp.bfloat16
F32 = jnp.float32


def split(x):
    high = x.astype(BF16)
    return high, (x - high.astype(F32)).astype(BF16)


def dft_rows(n_time, bins):
    times = jnp.arange(n_time, dtype=jnp.int32)
    phase = bins[:, None] * times[None, :] % n_time
    angle = phase.astype(F32) * (2.0 * math.pi / n_time)
    both = jnp.stack([jnp.cos(angle), -jnp.sin(angle)], axis=1)
    return both.reshape(-1, n_time) * (1.0 / math.sqrt(n_time))


def transform_kernel(sizes, table_ref, traces_ref, *refs):
    outs, scratch = refs[:-1], refs[-1]
    rows, step = sum(sizes), traces_ref.shape[0]
    contract = (((1,), (1,)), ((), ()))
    table_high, table_low = split(table_ref[...])
    table = jnp.concatenate([table_high, table_low])
    for s in range(step):
        high, low = split(traces_ref[s])
        both = lax.dot_general(table, high, contract, preferred_element_type=F32)
        rest = lax.dot_general(table_high, low, contract, preferred_element_type=F32)
        total = both[:rows] + (both[rows:] + rest)
        for lane in range(scratch.shape[0]):
            scratch[lane, pl.ds(s, rows, stride=step), :] = total[:, lane * 128 : (lane + 1) * 128]
    at = 0
    for size, out in zip(sizes, outs):
        for lane in range(scratch.shape[0]):
            block = scratch[lane, at * step : (at + size) * step, :]
            out[:, :, lane * 128 : (lane + 1) * 128] = block.reshape(size, step, 128)
        at += size


def transform(traces, table, sizes):
    n_src, n_rcv, n_time = traces.shape
    rows, step = sum(sizes), 8
    return pl.pallas_call(
        functools.partial(transform_kernel, sizes),
        grid=(n_src // step,),
        in_specs=[
            pl.BlockSpec((rows, n_time), lambda i: (0, 0)),
            pl.BlockSpec((step, n_rcv, n_time), lambda i: (i, 0, 0)),
        ],
        out_specs=[pl.BlockSpec((n, step, n_rcv), lambda i: (0, i, 0)) for n in sizes],
        out_shape=[jax.ShapeDtypeStruct((n, n_src, n_rcv), F32) for n in sizes],
        scratch_shapes=[pltpu.VMEM((n_rcv // 128, rows * step, 128), F32)],
        compiler_params=pltpu.CompilerParams(vmem_limit_bytes=48 << 20),
        cost_estimate=pl.CostEstimate(
            flops=6 * rows * n_src * n_rcv * n_time,
            bytes_accessed=4 * traces.size + 4 * rows * n_src * n_rcv,
            transcendentals=0,
        ),
    )(table, traces)


def product_kernel(scale, n_freq, n_src, n_rcv, place_ref, *refs):
    lefts = refs[: n_rcv * n_freq]
    rights = refs[n_rcv * n_freq : (n_rcv + n_src - 1) * n_freq]
    out, l_high, l_low, r_high, r_low = refs[-5:]
    freq, src, rcv = place_ref[0], place_ref[1], place_ref[2]
    _, height, width = lefts[0].shape
    rows = n_freq * height

    def put(high_ref, low_ref, top, left, block):
        high, low = split(block[...])
        where = (slice(None), pl.ds(pl.multiple_of(top, height), height), pl.ds(pl.multiple_of(left, 128), width))
        high_ref[where] = high
        low_ref[where] = low

    for peer in range(n_rcv):
        for d in range(n_freq):
            put(l_high, l_low, (freq ^ d) * height, (rcv ^ peer) * width, lefts[peer * n_freq + d])
    for peer in range(n_src):
        for d in range(n_freq):
            block = lefts[d] if peer == 0 else rights[(peer - 1) * n_freq + d]
            put(r_high, r_low, (src ^ peer) * rows + (freq ^ d) * height, 0, block)

    tile = min(256, rows)

    def dot(a, b):
        return jnp.dot(a, b, preferred_element_type=F32)

    def product(at, i, j):
        m = pl.ds(at, tile)
        return (
            dot(l_high[i, m, :], r_low[j])
            + dot(l_low[i, m, :], r_high[j])
            + dot(l_high[i, m, :], r_high[j])
        )

    for step in range(rows // tile):
        at = step * tile
        out[0, 0, pl.ds(at, tile), :] = scale * (product(at, 0, 0) - product(at, 1, 1))
        out[1, 0, pl.ds(at, tile), :] = scale * (product(at, 0, 1) + product(at, 1, 0))


def product(place, f, lefts, rights, done, mesh_sizes, scale):
    n_freq, n_src, n_rcv = mesh_sizes
    blocks = lefts + rights
    height, width = blocks[0][0].shape[1:]
    rows, inner = n_freq * height, n_src * n_freq * height

    def spec(at):
        return pl.BlockSpec((2, height, width), lambda i, place: (at, 0, 0))

    in_specs = [spec(at) for _, at in blocks]
    operands = [array for array, _ in blocks]
    alias = {}
    if done is not None:
        in_specs.append(pl.BlockSpec(memory_space=pl.ANY))
        operands.append(done)
        alias = {len(operands): 0}
    return pl.pallas_call(
        functools.partial(product_kernel, scale, n_freq, n_src, n_rcv),
        grid_spec=pltpu.PrefetchScalarGridSpec(
            num_scalar_prefetch=1,
            grid=(1,),
            in_specs=in_specs,
            out_specs=pl.BlockSpec((2, 1, rows, width), lambda i, place: (0, f, 0, 0)),
            scratch_shapes=[
                pltpu.VMEM((2, rows, inner), BF16),
                pltpu.VMEM((2, rows, inner), BF16),
                pltpu.VMEM((2, inner, width), BF16),
                pltpu.VMEM((2, inner, width), BF16),
            ],
        ),
        out_shape=jax.ShapeDtypeStruct((2, FPD, rows, width), F32),
        input_output_aliases=alias,
        compiler_params=pltpu.CompilerParams(vmem_limit_bytes=48 << 20),
        cost_estimate=pl.CostEstimate(
            flops=24 * rows * inner * width,
            bytes_accessed=4 * 2 * (rows * inner + inner * width + rows * width),
            transcendentals=0,
        ),
    )(place, *operands)


def per_device(traces):
    n_freq, n_src, n_rcv = (lax.axis_size(a) for a in ("freq", "src", "rcv"))
    freq = lax.axis_index("freq")
    place = jnp.stack([freq, lax.axis_index("src"), lax.axis_index("rcv")]).astype(jnp.int32)
    scale = -1.0 / math.sqrt(traces.shape[0] * n_freq * n_src)
    half = n_freq // 2

    pieces = [(d, tuple(range(FPD))) for d in range(half)]
    pieces += [(d, (f,)) for f in range(FPD) for d in range(half, n_freq)]
    bins = jnp.stack([(freq ^ d) * FPD + f for d, fs in pieces for f in fs])
    spectra = transform(traces, dft_rows(traces.shape[2], bins), [2 * len(fs) for _, fs in pieces])

    order = []

    def send(x, axis, d):
        if len(order) >= WINDOW:
            x, _ = lax.optimization_barrier((x, order[-WINDOW]))
        size = lax.axis_size(axis)
        y = lax.ppermute(x, axis, [(i, i ^ d) for i in range(size)])
        order.append(y)
        return y

    arrived, lefts, rights = {}, {}, {}

    def over_freq(p):
        d, _ = pieces[p]
        arrived[p] = send(spectra[p], "freq", d) if d else spectra[p]

    def onward(p):
        d, fs = pieces[p]
        peers = [arrived[p]] + [send(arrived[p], "rcv", e) for e in range(1, n_rcv)]
        others = [send(arrived[p], "src", e) for e in range(1, n_src)]
        for at, f in enumerate(fs):
            for e in range(n_rcv):
                lefts[f, e, d] = (peers[e], at)
            for e in range(1, n_src):
                rights[f, e, d] = (others[e - 1], at)

    far = list(range(half, len(pieces)))
    near = list(range(half))
    done = far[:2]
    for p in far[:2]:
        over_freq(p)
    over_freq(0)
    waiting = []
    queue = []
    nears = near[1:]
    fars = far[2:]
    onward_list = [0]
    for p in near[1:]:
        over_freq(p)
        onward(onward_list.pop(0))
        onward_list.append(p)
        if fars:
            q = fars.pop(0)
            over_freq(q)
            queue.append(q)
    onward_list += far[:2]
    onward_list += queue
    while onward_list:
        if fars:
            q = fars.pop(0)
            over_freq(q)
            onward_list.append(q)
        onward(onward_list.pop(0))

    out = None
    for f in range(FPD):
        left = [lefts[f, e, d] for e in range(n_rcv) for d in range(n_freq)]
        right = [rights[f, e, d] for e in range(1, n_src) for d in range(n_freq)]
        out = product(place, f, left, right, out, (n_freq, n_src, n_rcv), scale)
    return out


def solution(mesh):
    in_specs = (P(("src", "freq"), "rcv", None),)
    out_specs = P(None, "freq", "src", "rcv")
    return jax.shard_map(
        per_device, mesh=mesh, in_specs=in_specs, out_specs=out_specs, check_vma=False
    )
```

time: 442 us -> 275 us (0.62)
  blocking collectives: 145 us -> 0 us
  matrix products: 97.3 us -> 0 us
  starting transfers between devices: 0.3 us -> 63.6 us
  Pallas kernels: 0 us -> 53.6 us
  waiting for transfers between devices: 171 us -> 133 us
  between operations: 13.2 us -> 0.26 us
  local copies, waits for them, and re-layouts: 11.2 us -> 22.9 us
    all_gather x4 -> x0, waiting for transfers between devices: 169 us -> none  [the longest x1 77.5 us: per_device(): lax.all_gather(local_im, 'src', axis=1, tiled=True)]
    all_to_all x1 -> x0, blocking collectives: 145 us -> none  [per_device(): lax.all_to_all(spectra, 'freq', split_axis=0, concat_axis=1, tiled=True)]
    ppermute x0 -> x47, waiting for transfers between devices: none -> 133 us  [send(): y = lax.ppermute(x, axis, [(i, i ^ d) for i in range(size)])]
    dot_general x5 -> x0, matrix products: 97.3 us -> none  [the longest x4 56.6 us: batched_dot(): jnp.einsum('mgq,mqn->mgn', left, right, precision=lax.Precision.HIGHEST,...]
    ppermute x0 -> x47, starting transfers between devices: none -> 63.6 us  [send(): y = lax.ppermute(x, axis, [(i, i ^ d) for i in range(size)])]
    pallas_call x0 -> x4, Pallas kernels: none -> 53.6 us  [the longest x3 35.8 us: product(): pl.pallas_call(functools.partial(product_kernel, scale, n_freq, n_src, n_...]
    unnamed x5 -> x86, local copies, waits for them, and re-layouts: 3.47 us -> 22.7 us
    dot_general x1 -> x0, local copies, waits for them, and re-layouts: 6.43 us -> none  [per_device(): jnp.einsum('srt,tk->ksr', traces, dft_table, precision=lax.Precision.HIGH...]
  transfers between devices with their start and end apart: 4 -> 47, of which waited for: 4 -> 16; matrix products, arithmetic and copies ran while one was open for 7% -> 0% of each run, Pallas kernels for 0% -> 9%
where the time goes in v1:
time: 275 us; the launch traced here: 274 us
  waiting for transfers between devices  133 us (48%)
  starting transfers between devices  63.6 us (23%)
  Pallas kernels  53.6 us (19%)
  local copies, waits for them, and re-layouts  22.9 us (8%)
    ppermute x47, waiting for transfers between devices, send(): y = lax.ppermute(x, axis, [(i, i ^ d) for i in range(size)])  133 us
    ppermute x47, starting transfers between devices, send(): y = lax.ppermute(x, axis, [(i, i ^ d) for i in range(size)])  63.6 us
    pallas_call x3, Pallas kernels, product(): pl.pallas_call(functools.partial(product_kernel, scale, n_freq, n_src, n_...  35.8 us
    unnamed x86, local copies, waits for them, and re-layouts  22.7 us
    pallas_call x1, Pallas kernels, transform(): pl.pallas_call(functools.partial(transform_kernel, sizes), grid=(n_src //...  17.9 us
  transfers between devices with their start and end apart: 47, of which 16 were waited for; matrix products, arithmetic and copies ran while one was open for 0% of the time, Pallas kernels for 9%

profile of v1, /device:TPU:0, one launch (start us, length us, event | category | flops | bytes accessed | tf_op | source)
XLA Modules:
  0.0 274.1 jit_solution(11840814453567997652)
XLA Ops:
  0.4 17.9 %shard_map.17 = (f32[6,64,512]{2,1,0:T(8,128)S(1)}, f32[6,64,512]{2,1,0:T(8,128)S(1)}, f32[6,64,512]{2,1,0:T(8,128)S(1)}, f32[6,64,512]{2,1,0:T(8,128)}, f32[2,6...) custom-call(f32[48,256]{1,0:T(8,128)S(1)} %mul.104.table_ref, ...), custom_call_target="tpu_custom_call" | custom-call | flops 2415919104 | bytes 39845888 | tf_op jit(solution)/shard_map/pallas_call | solution.py:54
  18.3 5.0 %collective-permute-start.1 = (f32[2,64,512]{2,1,0:T(8,128)S(1)}, f32[2,64,512]{2,1,0:T(8,128)S(1)}, u32[]{:S(2)}, u32[]{:S(2)}) collective-permute-start(f32[2,64,512]{2,1,0:T(8,128)S(1)} %get-tuple-element.66), channel_id=1, source_target_pairs={{0,20},{4,16},{8,28},{12,24},{16,4},{20,0},{24,12},{28,8},{1,21},{... | collective-permute-start | bytes 786440 | tf_op jit(solution)/shard_map/ppermute | solution.py:173
  23.8 11.5 %collective-permute-done.1.refs_5_ = f32[2,64,512]{2,1,0:T(8,128)S(1)} collective-permute-done((f32[2,64,512]{2,1,0:T(8,128)S(1)}, f32[2,64,512]{2,1,0:T(8,128)S(1)}, u32[]{:S(2)}, u32[]{:S(2)}) %collective-permute-start.1) | collective-permute-done | bytes 262176 | tf_op jit(solution)/shard_map/ppermute | solution.py:173
  35.9 3.5 %collective-permute-start.3 = (f32[2,64,512]{2,1,0:T(8,128)S(1)}, f32[2,64,512]{2,1,0:T(8,128)S(1)}, u32[]{:S(2)}, u32[]{:S(2)}) collective-permute-start(f32[2,64,512]{2,1,0:T(8,128)S(1)} %get-tuple-element.70), channel_id=1, source_target_pairs={{0,16},{4,20},{8,24},{12,28},{16,0},{20,4},{24,8},{28,12},{1,17},{... | collective-permute-start | bytes 786440 | tf_op jit(solution)/shard_map/ppermute | solution.py:173
  39.3 19.1 %collective-permute-done.3.refs_4_ = f32[2,64,512]{2,1,0:T(8,128)S(1)} collective-permute-done((f32[2,64,512]{2,1,0:T(8,128)S(1)}, f32[2,64,512]{2,1,0:T(8,128)S(1)}, u32[]{:S(2)}, u32[]{:S(2)}) %collective-permute-start.3) | collective-permute-done | bytes 262176 | tf_op jit(solution)/shard_map/ppermute | solution.py:173
  58.5 3.1 %collective-permute-start.4 = (f32[2,64,512]{2,1,0:T(8,128)S(1)}, f32[2,64,512]{2,1,0:T(8,128)S(1)}, u32[]{:S(2)}, u32[]{:S(2)}) collective-permute-start(f32[2,64,512]{2,1,0:T(8,128)S(1)} %get-tuple-element.71), channel_id=1, source_target_pairs={{0,24},{4,28},{8,16},{12,20},{16,8},{20,12},{24,0},{28,4},{1,25},{... | collective-permute-start | bytes 786440 | tf_op jit(solution)/shard_map/ppermute | solution.py:173
  63.1 4.7 %collective-permute-done.4.refs_6_ = f32[2,64,512]{2,1,0:T(8,128)S(1)} collective-permute-done((f32[2,64,512]{2,1,0:T(8,128)S(1)}, f32[2,64,512]{2,1,0:T(8,128)S(1)}, u32[]{:S(2)}, u32[]{:S(2)}) %collective-permute-start.4) | collective-permute-done | bytes 262176 | tf_op jit(solution)/shard_map/ppermute | solution.py:173
  67.8 7.0 %collective-permute-start.5 = (f32[6,64,512]{2,1,0:T(8,128)}, f32[6,64,512]{2,1,0:T(8,128)S(1)}, u32[]{:S(2)}, u32[]{:S(2)}) collective-permute-start(f32[6,64,512]{2,1,0:T(8,128)} %get-tuple-element.72), channel_id=1, source_target_pairs={{0,12},{4,8},{8,4},{12,0},{16,28},{20,24},{24,20},{28,16},{1,13},{... | collective-permute-start | bytes 2359304 | tf_op jit(solution)/shard_map/ppermute | solution.py:173
  76.8 5.2 %collective-permute-done.15.refs_16_ = f32[6,64,512]{2,1,0:T(8,128)S(1)} collective-permute-done((f32[6,64,512]{2,1,0:T(8,128)S(1)}, f32[6,64,512]{2,1,0:T(8,128)S(1)}, u32[]{:S(2)}, u32[]{:S(2)}) %collective-permute-start.15) | collective-permute-done | bytes 786464 | tf_op jit(solution)/shard_map/ppermute | solution.py:173
  82.0 16.5 %collective-permute-done.5.refs_3_ = f32[6,64,512]{2,1,0:T(8,128)S(1)} collective-permute-done((f32[6,64,512]{2,1,0:T(8,128)}, f32[6,64,512]{2,1,0:T(8,128)S(1)}, u32[]{:S(2)}, u32[]{:S(2)}) %collective-permute-start.5) | collective-permute-done | bytes 786464 | tf_op jit(solution)/shard_map/ppermute | solution.py:173
  100.6 5.9 %collective-permute-done.16.refs_7_ = f32[2,64,512]{2,1,0:T(8,128)S(1)} collective-permute-done((f32[2,64,512]{2,1,0:T(8,128)S(1)}, f32[2,64,512]{2,1,0:T(8,128)S(1)}, u32[]{:S(2)}, u32[]{:S(2)}) %collective-permute-start.16) | collective-permute-done | bytes 262176 | tf_op jit(solution)/shard_map/ppermute | solution.py:173
  106.5 3.8 %collective-permute-start.8 = (f32[2,64,512]{2,1,0:T(8,128)S(1)}, f32[2,64,512]{2,1,0:T(8,128)S(1)}, u32[]{:S(2)}, u32[]{:S(2)}) collective-permute-start(f32[2,64,512]{2,1,0:T(8,128)S(1)} %get-tuple-element.76), channel_id=1, source_target_pairs={{0,16},{4,20},{8,24},{12,28},{16,0},{20,4},{24,8},{28,12},{1,17},{... | collective-permute-start | bytes 786440 | tf_op jit(solution)/shard_map/ppermute | solution.py:173
  110.4 14.9 %collective-permute-done.17.refs_5_ = f32[2,64,512]{2,1,0:T(8,128)S(1)} collective-permute-done((f32[2,64,512]{2,1,0:T(8,128)S(1)}, f32[2,64,512]{2,1,0:T(8,128)S(1)}, u32[]{:S(2)}, u32[]{:S(2)}) %collective-permute-start.17) | collective-permute-done | bytes 262176 | tf_op jit(solution)/shard_map/ppermute | solution.py:173
  126.8 3.1 %collective-permute-done.8.refs_4_ = f32[2,64,512]{2,1,0:T(8,128)S(1)} collective-permute-done((f32[2,64,512]{2,1,0:T(8,128)S(1)}, f32[2,64,512]{2,1,0:T(8,128)S(1)}, u32[]{:S(2)}, u32[]{:S(2)}) %collective-permute-start.8) | collective-permute-done | bytes 262176 | tf_op jit(solution)/shard_map/ppermute | solution.py:173
  130.6 10.4 %collective-permute-done.18.refs_20_ = f32[2,64,512]{2,1,0:T(8,128)S(1)} collective-permute-done((f32[2,64,512]{2,1,0:T(8,128)S(1)}, f32[2,64,512]{2,1,0:T(8,128)S(1)}, u32[]{:S(2)}, u32[]{:S(2)}) %collective-permute-start.18) | collective-permute-done | bytes 262176 | tf_op jit(solution)/shard_map/ppermute | solution.py:173
  141.7 3.2 %collective-permute-start.33 = (f32[2,64,512]{2,1,0:T(8,128)S(1)}, f32[2,64,512]{2,1,0:T(8,128)}, u32[]{:S(2)}, u32[]{:S(2)}) collective-permute-start(f32[2,64,512]{2,1,0:T(8,128)S(1)} %get-tuple-element.107), channel_id=1, source_target_pairs={{0,28},{4,24},{8,20},{12,16},{16,12},{20,8},{24,4},{28,0},{1,29},{... | collective-permute-start | bytes 786440 | tf_op jit(solution)/shard_map/ppermute | solution.py:173
  147.2 3.2 %collective-permute-start.23 = (f32[2,64,512]{2,1,0:T(8,128)S(1)}, f32[2,64,512]{2,1,0:T(8,128)}, u32[]{:S(2)}, u32[]{:S(2)}) collective-permute-start(f32[2,64,512]{2,1,0:T(8,128)S(1)} %get-tuple-element.96), channel_id=1, source_target_pairs={{0,24},{4,28},{8,16},{12,20},{16,8},{20,12},{24,0},{28,4},{1,25},{... | collective-permute-start | bytes 786440 | tf_op jit(solution)/shard_map/ppermute | solution.py:173
  156.0 24.4 %collective-permute-done.10.refs_4_ = f32[2,64,512]{2,1,0:T(8,128)S(1)} collective-permute-done((f32[2,64,512]{2,1,0:T(8,128)S(1)}, f32[2,64,512]{2,1,0:T(8,128)S(1)}, u32[]{:S(2)}, u32[]{:S(2)}) %collective-permute-start.10) | collective-permute-done | bytes 262176 | tf_op jit(solution)/shard_map/ppermute | solution.py:173
  183.8 8.4 %collective-permute-start.14 = (f32[2,64,512]{2,1,0:T(8,128)S(1)}, f32[2,64,512]{2,1,0:T(8,128)S(1)}, u32[]{:S(2)}, u32[]{:S(2)}) collective-permute-start(f32[2,64,512]{2,1,0:T(8,128)S(1)} %get-tuple-element.83), channel_id=1, source_target_pairs={{0,20},{4,16},{8,28},{12,24},{16,4},{20,0},{24,12},{28,8},{1,21},{... | collective-permute-start | bytes 786440 | tf_op jit(solution)/shard_map/ppermute | solution.py:173
  196.0 7.9 %collective-permute-done.14.refs_5_ = f32[2,64,512]{2,1,0:T(8,128)S(1)} collective-permute-done((f32[2,64,512]{2,1,0:T(8,128)S(1)}, f32[2,64,512]{2,1,0:T(8,128)S(1)}, u32[]{:S(2)}, u32[]{:S(2)}) %collective-permute-start.14) | collective-permute-done | bytes 262176 | tf_op jit(solution)/shard_map/ppermute | solution.py:173
  220.4 3.9 %collective-permute-done.31.refs_22_ = f32[2,64,512]{2,1,0:T(8,128)} collective-permute-done((f32[2,64,512]{2,1,0:T(8,128)}, f32[2,64,512]{2,1,0:T(8,128)}, u32[]{:S(2)}, u32[]{:S(2)}) %collective-permute-start.31) | collective-permute-done | bytes 262176 | tf_op jit(solution)/shard_map/ppermute | solution.py:173
  235.7 11.7 %shard_map.18.refs_24_ = f32[2,3,512,512]{3,2,1,0:T(8,128)} custom-call(s32[3]{0:T(128)S(1)} %pad_add_fusion.place_ref, f32[6,64,512]{2,1,0:T(8,128)S(1)} %get-tuple-element.63.refs_0_, f32[6,64,512]{2,1,0:T(8,128)S(1)} %collective-permute-done.refs_1_, f32[6,64,512]{2,1,0:T(8,128)S(1)} %collective-permute-done.2.refs_2_, f32[6,64,512]{2,1,0:T(8,128)} %copy-done.36, ...), custom_call_target="tpu_custom_call" | custom-call | flops 6442450944 | bytes 10485760 | tf_op jit(solution)/shard_map/pallas_call | solution.py:130
  249.9 12.3 %shard_map.19.refs_24_ = f32[2,3,512,512]{3,2,1,0:T(8,128)} custom-call(s32[3]{0:T(128)S(1)} %pad_add_fusion.place_ref, f32[6,64,512]{2,1,0:T(8,128)S(1)} %get-tuple-element.63.refs_0_, f32[6,64,512]{2,1,0:T(8,128)S(1)} %collective-permute-done.refs_1_, f32[6,64,512]{2,1,0:T(8,128)S(1)} %collective-permute-done.2.refs_2_, ...), custom_call_target="tpu_custom_call", output_to_operand_aliasing={{}: (25, {})} | custom-call | flops 6442450944 | bytes 10485760 | tf_op jit(solution)/shard_map/pallas_call | solution.py:130
  262.2 11.9 %shard_map.20 = f32[2,3,512,512]{3,2,1,0:T(8,128)} custom-call(s32[3]{0:T(128)S(1)} %pad_add_fusion.place_ref, f32[6,64,512]{2,1,0:T(8,128)S(1)} %get-tuple-element.63.refs_0_, f32[6,64,512]{2,1,0:T(8,128)S(1)} %collective-permute-done.refs_1_, f32[6,64,512]{2,1,0:T(8,128)S(1)} %collective-permute-done.2.refs_2_, ...), custom_call_target="tpu_custom_call", output_to_operand_aliasing={{}: (25, {})} | custom-call | flops 6442450944 | bytes 10485760 | tf_op jit(solution)/shard_map/pallas_call | solution.py:130
  (166 shorter events, 55.7 us)
Async XLA Ops:
  23.2 51.5 %collective-permute-start = (f32[6,64,512]{2,1,0:T(8,128)S(1)}, f32[6,64,512]{2,1,0:T(8,128)S(1)}, u32[]{:S(2)}, u32[]{:S(2)}) collective-permute-start(f32[6,64,512]{2,1,0:T(8,128)S(1)} %get-tuple-element.64), channel_id=1, source_target_pairs={{0,4},{4,0},{8,12},{12,8},{16,20},{20,16},{24,28},{28,24},{1,5},{5... | collective-permute-start | bytes 2359304 | tf_op jit(solution)/shard_map/ppermute | solution.py:173
  35.2 39.5 %collective-permute-start.2 = (f32[6,64,512]{2,1,0:T(8,128)S(1)}, f32[6,64,512]{2,1,0:T(8,128)S(1)}, u32[]{:S(2)}, u32[]{:S(2)}) collective-permute-start(f32[6,64,512]{2,1,0:T(8,128)S(1)} %get-tuple-element.67), channel_id=1, source_target_pairs={{0,8},{4,12},{8,0},{12,4},{16,24},{20,28},{24,16},{28,20},{1,9},{5... | collective-permute-start | bytes 2359304 | tf_op jit(solution)/shard_map/ppermute | solution.py:173
  35.9 22.6 %collective-permute-start.3 = (f32[2,64,512]{2,1,0:T(8,128)S(1)}, f32[2,64,512]{2,1,0:T(8,128)S(1)}, u32[]{:S(2)}, u32[]{:S(2)}) collective-permute-start(f32[2,64,512]{2,1,0:T(8,128)S(1)} %get-tuple-element.70), channel_id=1, source_target_pairs={{0,16},{4,20},{8,24},{12,28},{16,0},{20,4},{24,8},{28,12},{1,17},{... | collective-permute-start | bytes 786440 | tf_op jit(solution)/shard_map/ppermute | solution.py:173
  39.3 35.9 %collective-permute-start.6 = (f32[6,64,512]{2,1,0:T(8,128)S(1)}, f32[6,64,512]{2,1,0:T(8,128)S(1)}, u32[]{:S(2)}, u32[]{:S(2)}) collective-permute-start(f32[6,64,512]{2,1,0:T(8,128)S(1)} %get-tuple-element.63.refs_0_), channel_id=1, source_target_pairs={{0,1},{1,0},{2,3},{3,2},{4,5},{5,4},{6,7},{7,6},{8,9},{9,8},{10,11... | collective-permute-start | bytes 2359304 | tf_op jit(solution)/shard_map/ppermute | solution.py:173
  61.5 20.5 %collective-permute-start.15 = (f32[6,64,512]{2,1,0:T(8,128)S(1)}, f32[6,64,512]{2,1,0:T(8,128)S(1)}, u32[]{:S(2)}, u32[]{:S(2)}) collective-permute-start(f32[6,64,512]{2,1,0:T(8,128)S(1)} %get-tuple-element.63.refs_0_), channel_id=1, source_target_pairs={{0,2},{2,0},{1,3},{3,1},{4,6},{6,4},{5,7},{7,5},{8,10},{10,8},{9,1... | collective-permute-start | bytes 2359304 | tf_op jit(solution)/shard_map/ppermute | solution.py:173
  67.8 30.8 %collective-permute-start.5 = (f32[6,64,512]{2,1,0:T(8,128)}, f32[6,64,512]{2,1,0:T(8,128)S(1)}, u32[]{:S(2)}, u32[]{:S(2)}) collective-permute-start(f32[6,64,512]{2,1,0:T(8,128)} %get-tuple-element.72), channel_id=1, source_target_pairs={{0,12},{4,8},{8,4},{12,0},{16,28},{20,24},{24,20},{28,16},{1,13},{... | collective-permute-start | bytes 2359304 | tf_op jit(solution)/shard_map/ppermute | solution.py:173
  74.7 23.8 %collective-permute-start.21 = (f32[6,64,512]{2,1,0:T(8,128)S(1)}, f32[6,64,512]{2,1,0:T(8,128)S(1)}, u32[]{:S(2)}, u32[]{:S(2)}) collective-permute-start(f32[6,64,512]{2,1,0:T(8,128)S(1)} %collective-permute-done.refs_1_), channel_id=1, source_target_pairs={{0,1},{1,0},{2,3},{3,2},{4,5},{5,4},{6,7},{7,6},{8,9},{9,8},{10,11... | collective-permute-start | bytes 2359304 | tf_op jit(solution)/shard_map/ppermute | solution.py:173
  74.7 25.4 %collective-permute-start.11 = (f32[6,64,512]{2,1,0:T(8,128)S(1)}, f32[6,64,512]{2,1,0:T(8,128)S(1)}, u32[]{:S(2)}, u32[]{:S(2)}) collective-permute-start(f32[6,64,512]{2,1,0:T(8,128)S(1)} %collective-permute-done.2.refs_2_), channel_id=1, source_target_pairs={{0,1},{1,0},{2,3},{3,2},{4,5},{5,4},{6,7},{7,6},{8,9},{9,8},{10,11... | collective-permute-start | bytes 2359304 | tf_op jit(solution)/shard_map/ppermute | solution.py:173
  75.2 31.3 %collective-permute-start.7 = (f32[6,64,512]{2,1,0:T(8,128)S(1)}, f32[6,64,512]{2,1,0:T(8,128)S(1)}, u32[]{:S(2)}, u32[]{:S(2)}) collective-permute-start(f32[6,64,512]{2,1,0:T(8,128)S(1)} %collective-permute-done.refs_1_), channel_id=1, source_target_pairs={{0,2},{2,0},{1,3},{3,1},{4,6},{6,4},{5,7},{7,5},{8,10},{10,8},{9,1... | collective-permute-start | bytes 2359304 | tf_op jit(solution)/shard_map/ppermute | solution.py:173
  82.0 24.5 %collective-permute-start.16 = (f32[2,64,512]{2,1,0:T(8,128)S(1)}, f32[2,64,512]{2,1,0:T(8,128)S(1)}, u32[]{:S(2)}, u32[]{:S(2)}) collective-permute-start(f32[2,64,512]{2,1,0:T(8,128)S(1)} %get-tuple-element.87), channel_id=1, source_target_pairs={{0,28},{4,24},{8,20},{12,16},{16,12},{20,8},{24,4},{28,0},{1,29},{... | collective-permute-start | bytes 786440 | tf_op jit(solution)/shard_map/ppermute | solution.py:173
  98.5 43.1 %collective-permute-start.27 = (f32[6,64,512]{2,1,0:T(8,128)S(1)}, f32[6,64,512]{2,1,0:T(8,128)S(1)}, u32[]{:S(2)}, u32[]{:S(2)}) collective-permute-start(f32[6,64,512]{2,1,0:T(8,128)S(1)} %collective-permute-done.5.refs_3_), channel_id=1, source_target_pairs={{0,1},{1,0},{2,3},{3,2},{4,5},{5,4},{6,7},{7,6},{8,9},{9,8},{10,11... | collective-permute-start | bytes 2359304 | tf_op jit(solution)/shard_map/ppermute | solution.py:173
  98.5 48.7 %collective-permute-start.22 = (f32[6,64,512]{2,1,0:T(8,128)S(1)}, f32[6,64,512]{2,1,0:T(8,128)S(1)}, u32[]{:S(2)}, u32[]{:S(2)}) collective-permute-start(f32[6,64,512]{2,1,0:T(8,128)S(1)} %collective-permute-done.2.refs_2_), channel_id=1, source_target_pairs={{0,2},{2,0},{1,3},{3,1},{4,6},{6,4},{5,7},{7,5},{8,10},{10,8},{9,1... | collective-permute-start | bytes 2359304 | tf_op jit(solution)/shard_map/ppermute | solution.py:173
  100.1 50.3 %collective-permute-start.12 = (f32[6,64,512]{2,1,0:T(8,128)S(1)}, f32[6,64,512]{2,1,0:T(8,128)S(1)}, u32[]{:S(2)}, u32[]{:S(2)}) collective-permute-start(f32[6,64,512]{2,1,0:T(8,128)S(1)} %collective-permute-done.5.refs_3_), channel_id=1, source_target_pairs={{0,2},{2,0},{1,3},{3,1},{4,6},{6,4},{5,7},{7,5},{8,10},{10,8},{9,1... | collective-permute-start | bytes 2359304 | tf_op jit(solution)/shard_map/ppermute | solution.py:173
  106.5 23.4 %collective-permute-start.8 = (f32[2,64,512]{2,1,0:T(8,128)S(1)}, f32[2,64,512]{2,1,0:T(8,128)S(1)}, u32[]{:S(2)}, u32[]{:S(2)}) collective-permute-start(f32[2,64,512]{2,1,0:T(8,128)S(1)} %get-tuple-element.76), channel_id=1, source_target_pairs={{0,16},{4,20},{8,24},{12,28},{16,0},{20,4},{24,8},{28,12},{1,17},{... | collective-permute-start | bytes 786440 | tf_op jit(solution)/shard_map/ppermute | solution.py:173
  145.6 34.7 %collective-permute-start.10 = (f32[2,64,512]{2,1,0:T(8,128)S(1)}, f32[2,64,512]{2,1,0:T(8,128)S(1)}, u32[]{:S(2)}, u32[]{:S(2)}) collective-permute-start(f32[2,64,512]{2,1,0:T(8,128)S(1)} %get-tuple-element.78), channel_id=1, source_target_pairs={{0,16},{4,20},{8,24},{12,28},{16,0},{20,4},{24,8},{28,12},{1,17},{... | collective-permute-start | bytes 786440 | tf_op jit(solution)/shard_map/ppermute | solution.py:173
  147.2 34.6 %collective-permute-start.23 = (f32[2,64,512]{2,1,0:T(8,128)S(1)}, f32[2,64,512]{2,1,0:T(8,128)}, u32[]{:S(2)}, u32[]{:S(2)}) collective-permute-start(f32[2,64,512]{2,1,0:T(8,128)S(1)} %get-tuple-element.96), channel_id=1, source_target_pairs={{0,24},{4,28},{8,16},{12,20},{16,8},{20,12},{24,0},{28,4},{1,25},{... | collective-permute-start | bytes 786440 | tf_op jit(solution)/shard_map/ppermute | solution.py:173
  150.4 32.7 %collective-permute-start.13 = (f32[2,64,512]{2,1,0:T(8,128)S(1)}, f32[2,64,512]{2,1,0:T(8,128)S(1)}, u32[]{:S(2)}, u32[]{:S(2)}) collective-permute-start(f32[2,64,512]{2,1,0:T(8,128)S(1)} %collective-permute-done.1.refs_5_), channel_id=1, source_target_pairs={{0,1},{1,0},{2,3},{3,2},{4,5},{5,4},{6,7},{7,6},{8,9},{9,8},{10,11... | collective-permute-start | bytes 786440 | tf_op jit(solution)/shard_map/ppermute | solution.py:173
  151.1 41.0 %collective-permute-start.20 = (f32[2,64,512]{2,1,0:T(8,128)S(1)}, f32[2,64,512]{2,1,0:T(8,128)S(1)}, u32[]{:S(2)}, u32[]{:S(2)}) collective-permute-start(f32[2,64,512]{2,1,0:T(8,128)S(1)} %get-tuple-element.91), channel_id=1, source_target_pairs={{0,24},{4,28},{8,16},{12,20},{16,8},{20,12},{24,0},{28,4},{1,25},{... | collective-permute-start | bytes 786440 | tf_op jit(solution)/shard_map/ppermute | solution.py:173
  153.7 39.0 %collective-permute-start.38 = (f32[2,64,512]{2,1,0:T(8,128)S(1)}, f32[2,64,512]{2,1,0:T(8,128)S(1)}, u32[]{:S(2)}, u32[]{:S(2)}) collective-permute-start(f32[2,64,512]{2,1,0:T(8,128)S(1)} %collective-permute-done.4.refs_6_), channel_id=1, source_target_pairs={{0,2},{2,0},{1,3},{3,1},{4,6},{6,4},{5,7},{7,5},{8,10},{10,8},{9,1... | collective-permute-start | bytes 786440 | tf_op jit(solution)/shard_map/ppermute | solution.py:173
  215.2 47.0 %collective-permute-start.45 = (f32[2,64,512]{2,1,0:T(8,128)S(1)}, f32[2,64,512]{2,1,0:T(8,128)S(1)}, u32[]{:S(2)}, u32[]{:S(2)}) collective-permute-start(f32[2,64,512]{2,1,0:T(8,128)S(1)} %collective-permute-done.20.refs_6_), channel_id=1, source_target_pairs={{0,2},{2,0},{1,3},{3,1},{4,6},{6,4},{5,7},{7,5},{8,10},{10,8},{9,1... | collective-permute-start | bytes 786440 | tf_op jit(solution)/shard_map/ppermute | solution.py:173
  215.9 31.5 %collective-permute-start.41 = (f32[2,64,512]{2,1,0:T(8,128)S(1)}, f32[2,64,512]{2,1,0:T(8,128)S(1)}, u32[]{:S(2)}, u32[]{:S(2)}) collective-permute-start(f32[2,64,512]{2,1,0:T(8,128)S(1)} %collective-permute-done.10.refs_4_), channel_id=1, source_target_pairs={{0,2},{2,0},{1,3},{3,1},{4,6},{6,4},{5,7},{7,5},{8,10},{10,8},{9,1... | collective-permute-start | bytes 786440 | tf_op jit(solution)/shard_map/ppermute | solution.py:173
  218.7 43.5 %collective-permute-start.37 = (f32[2,64,512]{2,1,0:T(8,128)S(1)}, f32[2,64,512]{2,1,0:T(8,128)S(1)}, u32[]{:S(2)}, u32[]{:S(2)}) collective-permute-start(f32[2,64,512]{2,1,0:T(8,128)S(1)} %collective-permute-done.20.refs_6_), channel_id=1, source_target_pairs={{0,1},{1,0},{2,3},{3,2},{4,5},{5,4},{6,7},{7,6},{8,9},{9,8},{10,11... | collective-permute-start | bytes 786440 | tf_op jit(solution)/shard_map/ppermute | solution.py:173
  220.4 27.5 %collective-permute-start.43 = (f32[2,64,512]{2,1,0:T(8,128)}, f32[2,64,512]{2,1,0:T(8,128)S(1)}, u32[]{:S(2)}, u32[]{:S(2)}) collective-permute-start(f32[2,64,512]{2,1,0:T(8,128)} %collective-permute-done.33.refs_7_), channel_id=1, source_target_pairs={{0,1},{1,0},{2,3},{3,2},{4,5},{5,4},{6,7},{7,6},{8,9},{9,8},{10,11... | collective-permute-start | bytes 786440 | tf_op jit(solution)/shard_map/ppermute | solution.py:173
  224.3 24.9 %collective-permute-start.32 = (f32[2,64,512]{2,1,0:T(8,128)}, f32[2,64,512]{2,1,0:T(8,128)S(1)}, u32[]{:S(2)}, u32[]{:S(2)}) collective-permute-start(f32[2,64,512]{2,1,0:T(8,128)} %copy-done), channel_id=1, source_target_pairs={{0,1},{1,0},{2,3},{3,2},{4,5},{5,4},{6,7},{7,6},{8,9},{9,8},{10,11... | collective-permute-start | bytes 786440 | tf_op jit(solution)/shard_map/ppermute | solution.py:173
  (66 other events, 1265.0 us)

commit v2 on v1

v2 whole, which is shorter than its diff:
```python
import functools
import math

import jax
import jax.numpy as jnp
from jax import lax
from jax.experimental import pallas as pl
from jax.experimental.pallas import tpu as pltpu
from jax.sharding import PartitionSpec as P

FPD = 3
MIB = 1 << 20
EARLY = 2
BF16 = jnp.bfloat16
F32 = jnp.float32


def split(x):
    high = x.astype(BF16)
    return high, (x - high.astype(F32)).astype(BF16)


def dft_rows(n_time, bins):
    times = jnp.arange(n_time, dtype=jnp.int32)
    phase = bins[:, None] * times[None, :] % n_time
    angle = phase.astype(F32) * (2.0 * math.pi / n_time)
    both = jnp.stack([jnp.cos(angle), -jnp.sin(angle)], axis=1)
    return both.reshape(-1, n_time) * (1.0 / math.sqrt(n_time))


def transform_kernel(sizes, table_ref, traces_ref, *refs):
    outs, scratch = refs[:-1], refs[-1]
    rows, step = sum(sizes), traces_ref.shape[0]
    contract = (((1,), (1,)), ((), ()))
    table_high, table_low = split(table_ref[...])
    table = jnp.concatenate([table_high, table_low])
    for s in range(step):
        high, low = split(traces_ref[s])
        both = lax.dot_general(table, high, contract, preferred_element_type=F32)
        rest = lax.dot_general(table_high, low, contract, preferred_element_type=F32)
        total = both[:rows] + (both[rows:] + rest)
        for lane in range(scratch.shape[0]):
            scratch[lane, pl.ds(s, rows, stride=step), :] = total[:, lane * 128 : (lane + 1) * 128]
    at = 0
    for size, out in zip(sizes, outs):
        for lane in range(scratch.shape[0]):
            block = scratch[lane, at * step : (at + size) * step, :]
            out[:, :, lane * 128 : (lane + 1) * 128] = block.reshape(size, step, 128)
        at += size


def transform(traces, table, sizes):
    n_src, n_rcv, n_time = traces.shape
    rows, step = sum(sizes), 8
    return pl.pallas_call(
        functools.partial(transform_kernel, sizes),
        grid=(n_src // step,),
        in_specs=[
            pl.BlockSpec((rows, n_time), lambda i: (0, 0)),
            pl.BlockSpec((step, n_rcv, n_time), lambda i: (i, 0, 0)),
        ],
        out_specs=[pl.BlockSpec((n, step, n_rcv), lambda i: (0, i, 0)) for n in sizes],
        out_shape=[jax.ShapeDtypeStruct((n, n_src, n_rcv), F32) for n in sizes],
        scratch_shapes=[pltpu.VMEM((n_rcv // 128, rows * step, 128), F32)],
        compiler_params=pltpu.CompilerParams(vmem_limit_bytes=40 * MIB),
        cost_estimate=pl.CostEstimate(
            flops=6 * rows * n_src * n_rcv * n_time,
            bytes_accessed=4 * traces.size + 4 * rows * n_src * n_rcv,
            transcendentals=0,
        ),
    )(table, traces)


ANY = pl.BlockSpec(memory_space=pl.ANY)
CHEAP = pl.CostEstimate(flops=1, bytes_accessed=1, transcendentals=0)


def product_kernel(scale, f, natural, lefts_at, rights_at, sizes, n_in, place_ref, *refs):
    n_freq, n_src, n_rcv = sizes
    out = refs[n_in]
    left, right, l_high, l_low, r_high, r_low, result, sems, out_sems = refs[-9:]
    freq, src, rcv = place_ref[0], place_ref[1], place_ref[2]
    _, _, rows, width = left.shape
    height = rows // n_freq

    def fetch(target, blocks, n):
        copies = []
        for d, (array, first) in enumerate(blocks):
            top = d * height if natural else pl.multiple_of((freq ^ d) * height, height)
            copies.append(
                pltpu.make_async_copy(
                    refs[array].at[pl.ds(first, 2)], target.at[:, pl.ds(top, height)], sems.at[n + d]
                )
            )
            copies[-1].start()
        return copies

    copies = [fetch(left.at[e], lefts_at[e], e * n_freq) for e in range(n_rcv)]
    copies += [fetch(right.at[e], rights_at[e], (n_rcv + e) * n_freq) for e in range(n_src - 1)]

    for e in range(n_rcv):
        for copy in copies[e]:
            copy.wait()
        high, low = split(left[e])
        at = pl.ds(pl.multiple_of((rcv ^ e) * width, 128), width)
        l_high[:, :, at] = high
        l_low[:, :, at] = low
        if e == 0:
            at = pl.ds(pl.multiple_of(src * rows, rows), rows)
            r_high[:, at, :] = high
            r_low[:, at, :] = low
    for e in range(n_src - 1):
        for copy in copies[n_rcv + e]:
            copy.wait()
        high, low = split(right[e])
        at = pl.ds(pl.multiple_of((src ^ (e + 1)) * rows, rows), rows)
        r_high[:, at, :] = high
        r_low[:, at, :] = low

    tile = min(256, rows)

    def dot(a, b):
        return jnp.dot(a, b, preferred_element_type=F32)

    def part(m, i, j):
        return (
            dot(l_high[i, m, :], r_low[j])
            + dot(l_low[i, m, :], r_high[j])
            + dot(l_high[i, m, :], r_high[j])
        )

    copies = []
    for step in range(rows // tile):
        m = pl.ds(step * tile, tile)
        result[0, m, :] = scale * (part(m, 0, 0) - part(m, 1, 1))
        result[1, m, :] = scale * (part(m, 0, 1) + part(m, 1, 0))
        copies.append(pltpu.make_async_copy(result.at[:, m], out.at[:, f, m], out_sems.at[step]))
        copies[-1].start()
    for copy in copies:
        copy.wait()


def product(place, f, natural, lefts, rights, done, later, sizes, scale):
    n_freq, n_src, n_rcv = sizes
    height, width = lefts[0][0][0].shape[1:]
    rows, inner = n_freq * height, n_src * n_freq * height
    operands = []

    def place_of(blocks):
        found = []
        for array, first in blocks:
            known = [n for n, x in enumerate(operands) if x is array]
            if not known:
                operands.append(array)
            found.append((known[0] if known else len(operands) - 1, first))
        return found

    lefts_at, rights_at = [place_of(x) for x in lefts], [place_of(x) for x in rights]
    alias = {}
    shapes = [jax.ShapeDtypeStruct((2, FPD, rows, width), F32)]
    if done is not None:
        operands.append(done)
        alias[len(operands)] = 0
    for x in later:
        operands.append(x)
        alias[len(operands)] = len(shapes)
        shapes.append(jax.ShapeDtypeStruct(x.shape, x.dtype))
    return pl.pallas_call(
        functools.partial(product_kernel, scale, f, natural, lefts_at, rights_at, sizes, len(operands)),
        in_specs=[pl.BlockSpec(memory_space=pltpu.SMEM)] + [ANY] * len(operands),
        out_specs=[ANY] * len(shapes),
        out_shape=shapes,
        scratch_shapes=[
            pltpu.VMEM((n_rcv, 2, rows, width), F32),
            pltpu.VMEM((n_src - 1, 2, rows, width), F32),
            pltpu.VMEM((2, rows, inner), BF16),
            pltpu.VMEM((2, rows, inner), BF16),
            pltpu.VMEM((2, inner, width), BF16),
            pltpu.VMEM((2, inner, width), BF16),
            pltpu.VMEM((2, rows, width), F32),
            pltpu.SemaphoreType.DMA(((n_rcv + n_src - 1) * n_freq,)),
            pltpu.SemaphoreType.DMA((max(1, rows // 256),)),
        ],
        input_output_aliases=alias,
        compiler_params=pltpu.CompilerParams(vmem_limit_bytes=61 * MIB),
        cost_estimate=CHEAP
        if later
        else pl.CostEstimate(
            flops=24 * rows * inner * width,
            bytes_accessed=8 * (rows * inner + inner * width + rows * width),
            transcendentals=0,
        ),
    )(place, *operands)


def per_device(traces):
    n_freq, n_src, n_rcv = (lax.axis_size(a) for a in ("freq", "src", "rcv"))
    freq = lax.axis_index("freq")
    place = jnp.stack([freq, lax.axis_index("src"), lax.axis_index("rcv")]).astype(jnp.int32)
    scale = -1.0 / math.sqrt(traces.shape[0] * n_freq * n_src)
    half = n_freq // 2

    rest = FPD - 1
    sizes = (n_freq, n_src, n_rcv)

    pieces = [(d, tuple(range(1, FPD))) for d in range(half)]
    pieces += [(d, (f,)) for f in range(1, FPD) for d in range(half, n_freq)]
    bins = [jnp.arange(n_freq) * FPD] + [(freq ^ d) * FPD + jnp.array(fs) for d, fs in pieces]
    table = dft_rows(traces.shape[2], jnp.concatenate(bins))
    spectra = transform(traces, table, [2 * n_freq] + [2 * len(fs) for _, fs in pieces])
    whole, near, far = spectra[0], spectra[1 : half + 1], spectra[half + 1 :]

    def after(x, *others):
        return lax.optimization_barrier((x, *others))[0] if others else x

    def swap(x, axis, d, name):
        with jax.named_scope(name):
            return lax.ppermute(x, axis, [(i, i ^ d) for i in range(lax.axis_size(axis))])

    def to_src(x, name):
        return [swap(x, "src", e, name) for e in range(1, n_src)]

    def to_rcv(x, name):
        return [x] + [swap(x, "rcv", e, name) for e in range(1, n_rcv)]

    def every(x, first=0):
        return [(x, 2 * d) for d in range(n_freq)]

    first = lax.all_to_all(whole, "freq", split_axis=0, concat_axis=0, tiled=True)
    arrived, near_src = [near[0]], [to_src(near[0], "near_src_0")]

    def near_piece(d, *others):
        arrived.append(swap(after(near[d], *others), "freq", d, "near_freq_%d" % d))
        near_src.append(to_src(arrived[d], "near_src_%d" % d))

    for d in range(1, EARLY):
        near_piece(d)
    first_src = to_src(after(first, *[y for ys in near_src for y in ys]), "first_src")
    first_rcv = to_rcv(first, "first_rcv")
    for d in range(EARLY, half):
        near_piece(d, first)

    ready = [(0, True, [every(x) for x in first_rcv], [every(x) for x in first_src])]
    out = None
    before, ties = [first], [[]] * half
    for f in range(1, FPD):
        here, mine = [], list(far[(f - 1) * half : f * half])
        if f == FPD - 1:
            for done in ready[:-1]:
                out, mine[-1] = product(place, *done, out, [mine[-1]], sizes, scale)
        for i, x in enumerate(mine):
            here.append(swap(after(x, *before, *ties[i]), "freq", half + i, "far_freq_%d_%d" % (f, i)))
        far_src = [to_src(x, "far_src_%d_%d" % (f, i)) for i, x in enumerate(here)]
        own = [x[2 * (f - 1) : 2 * f] for x in arrived]
        x = jnp.concatenate(own + here)
        if f == FPD - 1:
            x = after(x, *[y for ys in far_src[: half // 2] for y in ys])
        gathered = to_rcv(x, "rcv_%d" % f)
        before = here + arrived[EARLY:] + first_src
        due = [y for ys in near_src[EARLY:] for y in ys] if f == 1 else []
        ties = [[] for _ in range(half)]
        for n, y in enumerate((due + [y for ys in far_src for y in ys])[: 2 * half - EARLY]):
            ties[min(1 + (n + 1) // 2, half - 1)].append(y)
        right = []
        for e in range(n_src - 1):
            right.append([(ys[e], 2 * (f - 1)) for ys in near_src] + [(ys[e], 0) for ys in far_src])
        ready.append((f, False, [every(x) for x in gathered], right))
    for done in ready[-2:]:
        out = product(place, *done, out, [], sizes, scale)[0]
    return out


def solution(mesh):
    in_specs = (P(("src", "freq"), "rcv", None),)
    out_specs = P(None, "freq", "src", "rcv")
    return jax.shard_map(
        per_device, mesh=mesh, in_specs=in_specs, out_specs=out_specs, check_vma=False
    )
```

time: 275 us -> 225 us (0.82)
  starting transfers between devices: 63.6 us -> 39.4 us
  waiting for transfers between devices: 133 us -> 115 us
  local copies, waits for them, and re-layouts: 22.9 us -> 15 us
    ppermute x47 -> x27, starting transfers between devices: 63.6 us -> 32.1 us  [swap(): lax.ppermute(x, axis, [(i, i ^ d) for i in range(lax.axis_size(axis))])]
    ppermute x47 -> x27, waiting for transfers between devices: 133 us -> 115 us  [swap(): lax.ppermute(x, axis, [(i, i ^ d) for i in range(lax.axis_size(axis))])]
    unnamed x86 -> x44, local copies, waits for them, and re-layouts: 22.7 us -> 13.4 us
    all_to_all x0 -> x1, starting transfers between devices: none -> 7.25 us  [per_device(): lax.all_to_all(whole, 'freq', split_axis=0, concat_axis=0, tiled=True)]
  transfers between devices with their start and end apart: 47 -> 28, of which waited for: 16 -> 12; matrix products, arithmetic and copies ran while one was open for 0% -> 5% of each run, Pallas kernels for 9% -> 11%
where the time goes in v2:
time: 225 us; the launch traced here: 224 us
  waiting for transfers between devices  115 us (51%)
  Pallas kernels  53.3 us (24%)
  starting transfers between devices  39.4 us (18%)
  local copies, waits for them, and re-layouts  15 us (7%)
    ppermute x27, waiting for transfers between devices, swap(): lax.ppermute(x, axis, [(i, i ^ d) for i in range(lax.axis_size(axis))])  115 us
    pallas_call x3, Pallas kernels, product(): pl.pallas_call(functools.partial(product_kernel, scale, f, natural, lefts...  35.6 us
    ppermute x27, starting transfers between devices, swap(): lax.ppermute(x, axis, [(i, i ^ d) for i in range(lax.axis_size(axis))])  32.1 us
    pallas_call x1, Pallas kernels, transform(): pl.pallas_call(functools.partial(transform_kernel, sizes), grid=(n_src //...  17.7 us
    unnamed x44, local copies, waits for them, and re-layouts  13.4 us
    all_to_all x1, starting transfers between devices, per_device(): lax.all_to_all(whole, 'freq', split_axis=0, concat_axis=0, tiled=True)  7.25 us
  transfers between devices with their start and end apart: 28, of which 12 were waited for; matrix products, arithmetic and copies ran while one was open for 5% of the time, Pallas kernels for 11%

profile of v2, /device:TPU:0, one launch (start us, length us, event | category | flops | bytes accessed | tf_op | source)
XLA Modules:
  0.0 224.5 jit_solution(6170890282552961768)
XLA Ops:
  1.0 17.7 %shard_map.127 = (f32[16,64,512]{2,1,0:T(8,128)}, f32[4,64,512]{2,1,0:T(8,128)S(1)}, f32[4,64,512]{2,1,0:T(8,128)S(1)}, f32[4,64,512]{2,1,0:T(8,128)S(1)}, f32[4...) custom-call(f32[48,256]{1,0:T(8,128)S(1)} %mul.96.table_ref, ...), custom_call_target="tpu_custom_call" | custom-call | flops 2415919104 | bytes 39845888 | tf_op jit(solution)/shard_map/pallas_call | solution.py:55
  20.9 7.3 %all-to-all-start = ((f32[16,64,512]{2,1,0:T(8,128)}), f32[16,64,512]{2,1,0:T(8,128)}, u32[]{:S(2)}, u32[]{:S(2)}) async-start(f32[16,64,512]{2,1,0:T(8,128)} %get-tuple-element.35), calls=%async_computation | async-start | bytes 4194304 | tf_op jit(solution)/shard_map/all_to_all | solution.py:229
  28.2 2.0 collective-permute-start
  31.7 32.5 %collective-permute-done = f32[4,64,512]{2,1,0:T(8,128)S(1)} collective-permute-done((f32[4,64,512]{2,1,0:T(8,128)S(1)}, f32[4,64,512]{2,1,0:T(8,128)S(1)}, u32[]{:S(2)}, u32[]{:S(2)}) %collective-permute-start) | collective-permute-done | bytes 524320 | tf_op jit(solution)/shard_map/near_freq_1/ppermute | solution.py:218
  66.5 10.0 %collective-permute-done.8.refs_3_ = f32[4,64,512]{2,1,0:T(8,128)S(1)} collective-permute-done((f32[4,64,512]{2,1,0:T(8,128)S(1)}, f32[4,64,512]{2,1,0:T(8,128)S(1)}, u32[]{:S(2)}, u32[]{:S(2)}) %collective-permute-start.8) | collective-permute-done | bytes 524320 | tf_op jit(solution)/shard_map/near_src_1/ppermute | solution.py:218
  76.6 1.5 collective-permute-start.9
  78.2 4.0 %collective-permute-start.3 = (f32[2,64,512]{2,1,0:T(8,128)}, f32[2,64,512]{2,1,0:T(8,128)S(1)}, u32[]{:S(2)}, u32[]{:S(2)}) collective-permute-start(f32[2,64,512]{2,1,0:T(8,128)} %copy-done.2), channel_id=1, source_target_pairs={{0,16},{4,20},{8,24},{12,28},{16,0},{20,4},{24,8},{28,12},{1,17},{... | collective-permute-start | bytes 786440 | tf_op jit(solution)/shard_map/far_freq_1_0/ppermute | solution.py:218
  83.1 13.1 %collective-permute-done.3 = f32[2,64,512]{2,1,0:T(8,128)S(1)} collective-permute-done((f32[2,64,512]{2,1,0:T(8,128)}, f32[2,64,512]{2,1,0:T(8,128)S(1)}, u32[]{:S(2)}, u32[]{:S(2)}) %collective-permute-start.3) | collective-permute-done | bytes 262176 | tf_op jit(solution)/shard_map/far_freq_1_0/ppermute | solution.py:218
  96.3 3.4 %collective-permute-start.5 = (f32[2,64,512]{2,1,0:T(8,128)S(1)}, f32[2,64,512]{2,1,0:T(8,128)S(1)}, u32[]{:S(2)}, u32[]{:S(2)}) collective-permute-start(f32[2,64,512]{2,1,0:T(8,128)S(1)} %get-tuple-element.45), channel_id=1, source_target_pairs={{0,24},{4,28},{8,16},{12,20},{16,8},{20,12},{24,0},{28,4},{1,25},{... | collective-permute-start | bytes 786440 | tf_op jit(solution)/shard_map/far_freq_1_2/ppermute | solution.py:218
  99.7 12.9 %collective-permute-done.4 = f32[2,64,512]{2,1,0:T(8,128)S(1)} collective-permute-done((f32[2,64,512]{2,1,0:T(8,128)}, f32[2,64,512]{2,1,0:T(8,128)S(1)}, u32[]{:S(2)}, u32[]{:S(2)}) %collective-permute-start.4) | collective-permute-done | bytes 262176 | tf_op jit(solution)/shard_map/far_freq_1_1/ppermute | solution.py:218
  114.1 2.5 %collective-permute-start.6 = (f32[2,64,512]{2,1,0:T(8,128)S(1)}, f32[2,64,512]{2,1,0:T(8,128)S(1)}, u32[]{:S(2)}, u32[]{:S(2)}) collective-permute-start(f32[2,64,512]{2,1,0:T(8,128)S(1)} %get-tuple-element.47), channel_id=1, source_target_pairs={{0,28},{4,24},{8,20},{12,16},{16,12},{20,8},{24,4},{28,0},{1,29},{... | collective-permute-start | bytes 786440 | tf_op jit(solution)/shard_map/far_freq_1_3/ppermute | solution.py:218
  116.6 1.9 slice_dynamic-update-slice_fusion.2
  119.3 15.9 %collective-permute-done.6 = f32[2,64,512]{2,1,0:T(8,128)S(1)} collective-permute-done((f32[2,64,512]{2,1,0:T(8,128)S(1)}, f32[2,64,512]{2,1,0:T(8,128)S(1)}, u32[]{:S(2)}, u32[]{:S(2)}) %collective-permute-start.6) | collective-permute-done | bytes 262176 | tf_op jit(solution)/shard_map/far_freq_1_3/ppermute | solution.py:218
  141.5 2.9 %collective-permute-done.14.refs_6_ = f32[2,64,512]{2,1,0:T(8,128)S(1)} collective-permute-done((f32[2,64,512]{2,1,0:T(8,128)S(1)}, f32[2,64,512]{2,1,0:T(8,128)S(1)}, u32[]{:S(2)}, u32[]{:S(2)}) %collective-permute-start.14) | collective-permute-done | bytes 262176 | tf_op jit(solution)/shard_map/far_src_1_0/ppermute | solution.py:218
  145.1 4.9 %collective-permute-done.17.refs_7_ = f32[2,64,512]{2,1,0:T(8,128)S(1)} collective-permute-done((f32[2,64,512]{2,1,0:T(8,128)S(1)}, f32[2,64,512]{2,1,0:T(8,128)S(1)}, u32[]{:S(2)}, u32[]{:S(2)}) %collective-permute-start.17) | collective-permute-done | bytes 262176 | tf_op jit(solution)/shard_map/far_src_1_1/ppermute | solution.py:218
  150.9 4.7 %collective-permute-done.18.refs_8_ = f32[2,64,512]{2,1,0:T(8,128)S(1)} collective-permute-done((f32[2,64,512]{2,1,0:T(8,128)S(1)}, f32[2,64,512]{2,1,0:T(8,128)S(1)}, u32[]{:S(2)}, u32[]{:S(2)}) %collective-permute-start.18) | collective-permute-done | bytes 262176 | tf_op jit(solution)/shard_map/far_src_1_2/ppermute | solution.py:218
  158.0 8.9 %collective-permute-done.13.refs_5_ = f32[4,64,512]{2,1,0:T(8,128)S(1)} collective-permute-done((f32[4,64,512]{2,1,0:T(8,128)S(1)}, f32[4,64,512]{2,1,0:T(8,128)S(1)}, u32[]{:S(2)}, u32[]{:S(2)}) %collective-permute-start.13) | collective-permute-done | bytes 524320 | tf_op jit(solution)/shard_map/near_src_3/ppermute | solution.py:218
  167.7 1.7 collective-permute-start.15
  170.0 11.8 %shard_map.128 = (f32[2,3,512,512]{3,2,1,0:T(8,128)}, f32[2,64,512]{2,1,0:T(8,128)}) custom-call(s32[3]{0:T(128)} %pad_add_fusion.place_ref, f32[16,64,512]{2,1,0:T(8,128)} %all-to-all-done.refs_0_, f32[16,64,512]{2,1,0:T(8,128)} %collective-permute-done.16.refs_1_, f32[16,64,512]{2,1,0:T(8,128)} %copy-done.3, ...), custom_call_target="tpu_custom_call", output_to_operand_aliasing={{1}: (4, {})} | custom-call | flops 1 | bytes 1 | tf_op jit(solution)/shard_map/pallas_call | solution.py:168
  181.8 2.0 collective-permute-start.20
  188.0 5.2 %collective-permute-done.20 = f32[2,64,512]{2,1,0:T(8,128)S(1)} collective-permute-done((f32[2,64,512]{2,1,0:T(8,128)}, f32[2,64,512]{2,1,0:T(8,128)S(1)}, u32[]{:S(2)}, u32[]{:S(2)}) %collective-permute-start.20) | collective-permute-done | bytes 262176 | tf_op jit(solution)/shard_map/far_freq_2_3/ppermute | solution.py:218
  194.0 3.5 %collective-permute-done.21.refs_6_ = f32[2,64,512]{2,1,0:T(8,128)S(1)} collective-permute-done((f32[2,64,512]{2,1,0:T(8,128)S(1)}, f32[2,64,512]{2,1,0:T(8,128)S(1)}, u32[]{:S(2)}, u32[]{:S(2)}) %collective-permute-start.21) | collective-permute-done | bytes 262176 | tf_op jit(solution)/shard_map/far_src_2_0/ppermute | solution.py:218
  199.5 12.0 %shard_map.129.refs_10_ = f32[2,3,512,512]{3,2,1,0:T(8,128)} custom-call(s32[3]{0:T(128)} %pad_add_fusion.place_ref, f32[16,64,512]{2,1,0:T(8,128)} %constant_dynamic-update-slice_fusion.4.refs_0_, f32[16,64,512]{2,1,0:T(8,128)} %collective-permute-done.26.refs_1_, f32[4,64,512]{2,1,0:T(8,128)} %copy-done.5, ...), custom_call_target="tpu_custom_call", output_to_operand_aliasing={{}: (11, {})} | custom-call | flops 6442450944 | bytes 10485760 | tf_op jit(solution)/shard_map/pallas_call | solution.py:168
  212.5 11.8 %shard_map.130 = f32[2,3,512,512]{3,2,1,0:T(8,128)} custom-call(s32[3]{0:T(128)} %pad_add_fusion.place_ref, f32[16,64,512]{2,1,0:T(8,128)} %constant_dynamic-update-slice_fusion.refs_0_, f32[16,64,512]{2,1,0:T(8,128)} %collective-permute-done.23.refs_1_, f32[4,64,512]{2,1,0:T(8,128)} %copy-done.5, ...), custom_call_target="tpu_custom_call", output_to_operand_aliasing={{}: (11, {})} | custom-call | flops 6442450944 | bytes 10485760 | tf_op jit(solution)/shard_map/pallas_call | solution.py:168
  (90 shorter events, 30.0 us)
Async XLA Ops:
  20.9 55.7 %all-to-all-start = ((f32[16,64,512]{2,1,0:T(8,128)}), f32[16,64,512]{2,1,0:T(8,128)}, u32[]{:S(2)}, u32[]{:S(2)}) async-start(f32[16,64,512]{2,1,0:T(8,128)} %get-tuple-element.35), calls=%async_computation | async-start | bytes 4194304 | tf_op jit(solution)/shard_map/all_to_all | solution.py:229
  28.2 36.1 %collective-permute-start = (f32[4,64,512]{2,1,0:T(8,128)S(1)}, f32[4,64,512]{2,1,0:T(8,128)S(1)}, u32[]{:S(2)}, u32[]{:S(2)}) collective-permute-start(f32[4,64,512]{2,1,0:T(8,128)S(1)} %get-tuple-element.33), channel_id=1, source_target_pairs={{0,4},{4,0},{8,12},{12,8},{16,20},{20,16},{24,28},{28,24},{1,5},{5... | collective-permute-start | bytes 1572872 | tf_op jit(solution)/shard_map/near_freq_1/ppermute | solution.py:218
  30.2 35.6 %collective-permute-start.7 = (f32[4,64,512]{2,1,0:T(8,128)S(1)}, f32[4,64,512]{2,1,0:T(8,128)S(1)}, u32[]{:S(2)}, u32[]{:S(2)}) collective-permute-start(f32[4,64,512]{2,1,0:T(8,128)S(1)} %get-tuple-element.32), channel_id=1, source_target_pairs={{0,2},{2,0},{1,3},{3,1},{4,6},{6,4},{5,7},{7,5},{8,10},{10,8},{9,1... | collective-permute-start | bytes 1572872 | tf_op jit(solution)/shard_map/near_src_0/ppermute | solution.py:218
  76.6 61.2 %collective-permute-start.9 = (f32[16,64,512]{2,1,0:T(8,128)}, f32[16,64,512]{2,1,0:T(8,128)S(1)}, u32[]{:S(2)}, u32[]{:S(2)}) collective-permute-start(f32[16,64,512]{2,1,0:T(8,128)} %all-to-all-done.refs_0_), channel_id=1, source_target_pairs={{0,2},{2,0},{1,3},{3,1},{4,6},{6,4},{5,7},{7,5},{8,10},{10,8},{9,1... | collective-permute-start | bytes 6291464 | tf_op jit(solution)/shard_map/first_src/ppermute | solution.py:218
  78.1 89.6 %collective-permute-start.16 = (f32[16,64,512]{2,1,0:T(8,128)}, f32[16,64,512]{2,1,0:T(8,128)}, u32[]{:S(2)}, u32[]{:S(2)}) collective-permute-start(f32[16,64,512]{2,1,0:T(8,128)} %all-to-all-done.refs_0_), channel_id=1, source_target_pairs={{0,1},{1,0},{2,3},{3,2},{4,5},{5,4},{6,7},{7,6},{8,9},{9,8},{10,11... | collective-permute-start | bytes 6291464 | tf_op jit(solution)/shard_map/first_rcv/ppermute | solution.py:218
  78.1 34.6 %collective-permute-start.1 = (f32[4,64,512]{2,1,0:T(8,128)S(1)}, f32[4,64,512]{2,1,0:T(8,128)S(1)}, u32[]{:S(2)}, u32[]{:S(2)}) collective-permute-start(f32[4,64,512]{2,1,0:T(8,128)S(1)} %get-tuple-element.36), channel_id=1, source_target_pairs={{0,8},{4,12},{8,0},{12,4},{16,24},{20,28},{24,16},{28,20},{1,9},{5... | collective-permute-start | bytes 1572872 | tf_op jit(solution)/shard_map/near_freq_2/ppermute | solution.py:218
  78.2 18.1 %collective-permute-start.3 = (f32[2,64,512]{2,1,0:T(8,128)}, f32[2,64,512]{2,1,0:T(8,128)S(1)}, u32[]{:S(2)}, u32[]{:S(2)}) collective-permute-start(f32[2,64,512]{2,1,0:T(8,128)} %copy-done.2), channel_id=1, source_target_pairs={{0,16},{4,20},{8,24},{12,28},{16,0},{20,4},{24,8},{28,12},{1,17},{... | collective-permute-start | bytes 786440 | tf_op jit(solution)/shard_map/far_freq_1_0/ppermute | solution.py:218
  82.1 30.4 %collective-permute-start.4 = (f32[2,64,512]{2,1,0:T(8,128)}, f32[2,64,512]{2,1,0:T(8,128)S(1)}, u32[]{:S(2)}, u32[]{:S(2)}) collective-permute-start(f32[2,64,512]{2,1,0:T(8,128)} %copy-done.1), channel_id=1, source_target_pairs={{0,20},{4,16},{8,28},{12,24},{16,4},{20,0},{24,12},{28,8},{1,21},{... | collective-permute-start | bytes 786440 | tf_op jit(solution)/shard_map/far_freq_1_1/ppermute | solution.py:218
  96.3 17.8 %collective-permute-start.5 = (f32[2,64,512]{2,1,0:T(8,128)S(1)}, f32[2,64,512]{2,1,0:T(8,128)S(1)}, u32[]{:S(2)}, u32[]{:S(2)}) collective-permute-start(f32[2,64,512]{2,1,0:T(8,128)S(1)} %get-tuple-element.45), channel_id=1, source_target_pairs={{0,24},{4,28},{8,16},{12,20},{16,8},{20,12},{24,0},{28,4},{1,25},{... | collective-permute-start | bytes 786440 | tf_op jit(solution)/shard_map/far_freq_1_2/ppermute | solution.py:218
  112.6 23.1 %collective-permute-start.2 = (f32[4,64,512]{2,1,0:T(8,128)S(1)}, f32[4,64,512]{2,1,0:T(8,128)S(1)}, u32[]{:S(2)}, u32[]{:S(2)}) collective-permute-start(f32[4,64,512]{2,1,0:T(8,128)S(1)} %get-tuple-element.38), channel_id=1, source_target_pairs={{0,12},{4,8},{8,4},{12,0},{16,28},{20,24},{24,20},{28,16},{1,13},{... | collective-permute-start | bytes 1572872 | tf_op jit(solution)/shard_map/near_freq_3/ppermute | solution.py:218
  112.7 24.5 %collective-permute-start.11 = (f32[4,64,512]{2,1,0:T(8,128)S(1)}, f32[4,64,512]{2,1,0:T(8,128)S(1)}, u32[]{:S(2)}, u32[]{:S(2)}) collective-permute-start(f32[4,64,512]{2,1,0:T(8,128)S(1)} %collective-permute-done.1), channel_id=1, source_target_pairs={{0,2},{2,0},{1,3},{3,1},{4,6},{6,4},{5,7},{7,5},{8,10},{10,8},{9,1... | collective-permute-start | bytes 1572872 | tf_op jit(solution)/shard_map/near_src_2/ppermute | solution.py:218
  114.1 21.1 %collective-permute-start.6 = (f32[2,64,512]{2,1,0:T(8,128)S(1)}, f32[2,64,512]{2,1,0:T(8,128)S(1)}, u32[]{:S(2)}, u32[]{:S(2)}) collective-permute-start(f32[2,64,512]{2,1,0:T(8,128)S(1)} %get-tuple-element.47), channel_id=1, source_target_pairs={{0,28},{4,24},{8,20},{12,16},{16,12},{20,8},{24,4},{28,0},{1,29},{... | collective-permute-start | bytes 786440 | tf_op jit(solution)/shard_map/far_freq_1_3/ppermute | solution.py:218
  135.7 14.3 %collective-permute-start.17 = (f32[2,64,512]{2,1,0:T(8,128)S(1)}, f32[2,64,512]{2,1,0:T(8,128)S(1)}, u32[]{:S(2)}, u32[]{:S(2)}) collective-permute-start(f32[2,64,512]{2,1,0:T(8,128)S(1)} %collective-permute-done.4), channel_id=1, source_target_pairs={{0,2},{2,0},{1,3},{3,1},{4,6},{6,4},{5,7},{7,5},{8,10},{10,8},{9,1... | collective-permute-start | bytes 786440 | tf_op jit(solution)/shard_map/far_src_1_1/ppermute | solution.py:218
  137.2 18.4 %collective-permute-start.18 = (f32[2,64,512]{2,1,0:T(8,128)S(1)}, f32[2,64,512]{2,1,0:T(8,128)S(1)}, u32[]{:S(2)}, u32[]{:S(2)}) collective-permute-start(f32[2,64,512]{2,1,0:T(8,128)S(1)} %collective-permute-done.5), channel_id=1, source_target_pairs={{0,2},{2,0},{1,3},{3,1},{4,6},{6,4},{5,7},{7,5},{8,10},{10,8},{9,1... | collective-permute-start | bytes 786440 | tf_op jit(solution)/shard_map/far_src_1_2/ppermute | solution.py:218
  137.7 29.2 %collective-permute-start.13 = (f32[4,64,512]{2,1,0:T(8,128)S(1)}, f32[4,64,512]{2,1,0:T(8,128)S(1)}, u32[]{:S(2)}, u32[]{:S(2)}) collective-permute-start(f32[4,64,512]{2,1,0:T(8,128)S(1)} %collective-permute-done.2), channel_id=1, source_target_pairs={{0,2},{2,0},{1,3},{3,1},{4,6},{6,4},{5,7},{7,5},{8,10},{10,8},{9,1... | collective-permute-start | bytes 1572872 | tf_op jit(solution)/shard_map/near_src_3/ppermute | solution.py:218
  144.4 37.3 %collective-permute-start.19 = (f32[2,64,512]{2,1,0:T(8,128)S(1)}, f32[2,64,512]{2,1,0:T(8,128)S(1)}, u32[]{:S(2)}, u32[]{:S(2)}) collective-permute-start(f32[2,64,512]{2,1,0:T(8,128)S(1)} %collective-permute-done.6), channel_id=1, source_target_pairs={{0,2},{2,0},{1,3},{3,1},{4,6},{6,4},{5,7},{7,5},{8,10},{10,8},{9,1... | collective-permute-start | bytes 786440 | tf_op jit(solution)/shard_map/far_src_1_3/ppermute | solution.py:218
  150.1 33.7 %collective-permute-start.12 = (f32[2,64,512]{2,1,0:T(8,128)S(1)}, f32[2,64,512]{2,1,0:T(8,128)S(1)}, u32[]{:S(2)}, u32[]{:S(2)}) collective-permute-start(f32[2,64,512]{2,1,0:T(8,128)S(1)} %get-tuple-element.51), channel_id=1, source_target_pairs={{0,20},{4,16},{8,28},{12,24},{16,4},{20,0},{24,12},{28,8},{1,21},{... | collective-permute-start | bytes 786440 | tf_op jit(solution)/shard_map/far_freq_2_1/ppermute | solution.py:218
  155.7 28.8 %collective-permute-start.10 = (f32[2,64,512]{2,1,0:T(8,128)S(1)}, f32[2,64,512]{2,1,0:T(8,128)S(1)}, u32[]{:S(2)}, u32[]{:S(2)}) collective-permute-start(f32[2,64,512]{2,1,0:T(8,128)S(1)} %get-tuple-element.49), channel_id=1, source_target_pairs={{0,16},{4,20},{8,24},{12,28},{16,0},{20,4},{24,8},{28,12},{1,17},{... | collective-permute-start | bytes 786440 | tf_op jit(solution)/shard_map/far_freq_2_0/ppermute | solution.py:218
  167.7 31.8 %collective-permute-start.26 = (f32[16,64,512]{2,1,0:T(8,128)}, f32[16,64,512]{2,1,0:T(8,128)}, u32[]{:S(2)}, u32[]{:S(2)}) collective-permute-start(f32[16,64,512]{2,1,0:T(8,128)} %constant_dynamic-update-slice_fusion.4.refs_0_), channel_id=1, source_target_pairs={{0,1},{1,0},{2,3},{3,2},{4,5},{5,4},{6,7},{7,6},{8,9},{9,8},{10,11... | collective-permute-start | bytes 6291464 | tf_op jit(solution)/shard_map/rcv_1/ppermute | solution.py:218
  167.7 19.5 %collective-permute-start.15 = (f32[2,64,512]{2,1,0:T(8,128)S(1)}, f32[2,64,512]{2,1,0:T(8,128)S(1)}, u32[]{:S(2)}, u32[]{:S(2)}) collective-permute-start(f32[2,64,512]{2,1,0:T(8,128)S(1)} %get-tuple-element.53), channel_id=1, source_target_pairs={{0,24},{4,28},{8,16},{12,20},{16,8},{20,12},{24,0},{28,4},{1,25},{... | collective-permute-start | bytes 786440 | tf_op jit(solution)/shard_map/far_freq_2_2/ppermute | solution.py:218
  184.4 13.0 %collective-permute-start.21 = (f32[2,64,512]{2,1,0:T(8,128)S(1)}, f32[2,64,512]{2,1,0:T(8,128)S(1)}, u32[]{:S(2)}, u32[]{:S(2)}) collective-permute-start(f32[2,64,512]{2,1,0:T(8,128)S(1)} %collective-permute-done.10), channel_id=1, source_target_pairs={{0,2},{2,0},{1,3},{3,1},{4,6},{6,4},{5,7},{7,5},{8,10},{10,8},{9,1... | collective-permute-start | bytes 786440 | tf_op jit(solution)/shard_map/far_src_2_0/ppermute | solution.py:218
  197.5 14.3 %collective-permute-start.23 = (f32[16,64,512]{2,1,0:T(8,128)}, f32[16,64,512]{2,1,0:T(8,128)}, u32[]{:S(2)}, u32[]{:S(2)}) collective-permute-start(f32[16,64,512]{2,1,0:T(8,128)} %constant_dynamic-update-slice_fusion.refs_0_), channel_id=1, source_target_pairs={{0,1},{1,0},{2,3},{3,2},{4,5},{5,4},{6,7},{7,6},{8,9},{9,8},{10,11... | collective-permute-start | bytes 6291464 | tf_op jit(solution)/shard_map/rcv_2/ppermute | solution.py:218
  197.5 14.1 %collective-permute-start.24 = (f32[2,64,512]{2,1,0:T(8,128)S(1)}, f32[2,64,512]{2,1,0:T(8,128)S(1)}, u32[]{:S(2)}, u32[]{:S(2)}) collective-permute-start(f32[2,64,512]{2,1,0:T(8,128)S(1)} %collective-permute-done.15), channel_id=1, source_target_pairs={{0,2},{2,0},{1,3},{3,1},{4,6},{6,4},{5,7},{7,5},{8,10},{10,8},{9,1... | collective-permute-start | bytes 786440 | tf_op jit(solution)/shard_map/far_src_2_2/ppermute | solution.py:218
  198.1 13.7 %collective-permute-start.25 = (f32[2,64,512]{2,1,0:T(8,128)S(1)}, f32[2,64,512]{2,1,0:T(8,128)S(1)}, u32[]{:S(2)}, u32[]{:S(2)}) collective-permute-start(f32[2,64,512]{2,1,0:T(8,128)S(1)} %collective-permute-done.20), channel_id=1, source_target_pairs={{0,2},{2,0},{1,3},{3,1},{4,6},{6,4},{5,7},{7,5},{8,10},{10,8},{9,1... | collective-permute-start | bytes 786440 | tf_op jit(solution)/shard_map/far_src_2_3/ppermute | solution.py:218
  (21 other events, 257.4 us)

commit v3 on v2

--- a/solution.py
+++ b/solution.py
@@ -62,7 +62,7 @@
         out_specs=[pl.BlockSpec((n, step, n_rcv), lambda i: (0, i, 0)) for n in sizes],
         out_shape=[jax.ShapeDtypeStruct((n, n_src, n_rcv), F32) for n in sizes],
         scratch_shapes=[pltpu.VMEM((n_rcv // 128, rows * step, 128), F32)],
-        compiler_params=pltpu.CompilerParams(vmem_limit_bytes=40 * MIB),
+        compiler_params=pltpu.CompilerParams(vmem_limit_bytes=32 * MIB),
         cost_estimate=pl.CostEstimate(
             flops=6 * rows * n_src * n_rcv * n_time,
             bytes_accessed=4 * traces.size + 4 * rows * n_src * n_rcv,
@@ -236,31 +236,42 @@
     for d in range(1, EARLY):
         near_piece(d)
     first_src = to_src(after(first, *[y for ys in near_src for y in ys]), "first_src")
-    first_rcv = to_rcv(first, "first_rcv")
     for d in range(EARLY, half):
         near_piece(d, first)
 
-    ready = [(0, True, [every(x) for x in first_rcv], [every(x) for x in first_src])]
-    out = None
+    ready, out = [], None
     before, ties = [first], [[]] * half
+    queue = [ys[-1] for ys in near_src[EARLY:]]
+    started = {}
+
+    def start(f, i, *others):
+        x = after(far[(f - 1) * half + i], *others)
+        started[f, i] = swap(x, "freq", half + i, "far_freq_%d_%d" % (f, i))
+        return started[f, i]
+
+    far = list(far)
     for f in range(1, FPD):
-        here, mine = [], list(far[(f - 1) * half : f * half])
         if f == FPD - 1:
+            first_rcv = [first] + to_rcv(after(first, *before), "first_rcv")[1:]
+            ready.insert(0, (0, True, [every(x) for x in first_rcv], [every(x) for x in first_src]))
             for done in ready[:-1]:
-                out, mine[-1] = product(place, *done, out, [mine[-1]], sizes, scale)
-        for i, x in enumerate(mine):
-            here.append(swap(after(x, *before, *ties[i]), "freq", half + i, "far_freq_%d_%d" % (f, i)))
-        far_src = [to_src(x, "far_src_%d_%d" % (f, i)) for i, x in enumerate(here)]
+                out, far[-1] = product(place, *done, out, [far[-1]], sizes, scale)
+        here = [started[f, i] if (f, i) in started else start(f, i, *before, *ties[i]) for i in range(half)]
+        before = here + arrived[EARLY:] + first_src
+        lead = [start(f + 1, i, *before) for i in range(half // 2)] if f < FPD - 1 else []
+        far_src = []
+        for i, x in enumerate(here):
+            held = queue[-2:-1] + lead[i : i + 1] if lead[i : i + 1] else []
+            far_src.append(to_src(after(x, *held), "far_src_%d_%d" % (f, i)))
+            queue.append(far_src[-1][-1])
         own = [x[2 * (f - 1) : 2 * f] for x in arrived]
         x = jnp.concatenate(own + here)
         if f == FPD - 1:
-            x = after(x, *[y for ys in far_src[: half // 2] for y in ys])
+            x = after(x, *queue[:-half], *[y for ys in far_src[: half // 2] for y in ys])
         gathered = to_rcv(x, "rcv_%d" % f)
-        before = here + arrived[EARLY:] + first_src
-        due = [y for ys in near_src[EARLY:] for y in ys] if f == 1 else []
         ties = [[] for _ in range(half)]
-        for n, y in enumerate((due + [y for ys in far_src for y in ys])[: 2 * half - EARLY]):
-            ties[min(1 + (n + 1) // 2, half - 1)].append(y)
+        ties[half - 2] = queue[:1]
+        ties[half - 1] = queue[1:]
         right = []
         for e in range(n_src - 1):
             right.append([(ys[e], 2 * (f - 1)) for ys in near_src] + [(ys[e], 0) for ys in far_src])

time: 225 us -> 221 us (0.982)
  waiting for transfers between devices: 115 us -> 105 us
  local copies, waits for them, and re-layouts: 15 us -> 18.8 us
    ppermute x27, waiting for transfers between devices: 115 us -> 105 us  [swap(): lax.ppermute(x, axis, [(i, i ^ d) for i in range(lax.axis_size(axis))])]
    unnamed x44 -> x46, local copies, waits for them, and re-layouts: 13.4 us -> 16.2 us
  transfers between devices with their start and end apart: 28 -> 28, of which waited for: 12 -> 13; matrix products, arithmetic and copies ran while one was open for 5% -> 7% of each run, Pallas kernels for 11% -> 11%
where the time goes in v3:
time: 221 us; the launch traced here: 220 us
  waiting for transfers between devices  105 us (48%)
  Pallas kernels  53.4 us (24%)
  starting transfers between devices  41.5 us (19%)
  local copies, waits for them, and re-layouts  18.8 us (9%)
    ppermute x27, waiting for transfers between devices, swap(): lax.ppermute(x, axis, [(i, i ^ d) for i in range(lax.axis_size(axis))])  105 us
    pallas_call x3, Pallas kernels, product(): pl.pallas_call(functools.partial(product_kernel, scale, f, natural, lefts...  35.7 us
    ppermute x27, starting transfers between devices, swap(): lax.ppermute(x, axis, [(i, i ^ d) for i in range(lax.axis_size(axis))])  34.3 us
    pallas_call x1, Pallas kernels, transform(): pl.pallas_call(functools.partial(transform_kernel, sizes), grid=(n_src //...  17.7 us
    unnamed x46, local copies, waits for them, and re-layouts  16.2 us
    all_to_all x1, starting transfers between devices, per_device(): lax.all_to_all(whole, 'freq', split_axis=0, concat_axis=0, tiled=True)  7.25 us
  transfers between devices with their start and end apart: 28, of which 13 were waited for; matrix products, arithmetic and copies ran while one was open for 7% of the time, Pallas kernels for 11%

profile of v3, /device:TPU:0, one launch (start us, length us, event | category | flops | bytes accessed | tf_op | source)
XLA Modules:
  0.0 220.1 jit_solution(6135230886988556755)
XLA Ops:
  1.0 17.7 %shard_map.127 = (f32[16,64,512]{2,1,0:T(8,128)}, f32[4,64,512]{2,1,0:T(8,128)S(1)}, f32[4,64,512]{2,1,0:T(8,128)S(1)}, f32[4,64,512]{2,1,0:T(8,128)S(1)}, f32[4...) custom-call(f32[48,256]{1,0:T(8,128)S(1)} %mul.96.table_ref, ...), custom_call_target="tpu_custom_call" | custom-call | flops 2415919104 | bytes 39845888 | tf_op jit(solution)/shard_map/pallas_call | solution.py:55
  20.9 7.3 %all-to-all-start = ((f32[16,64,512]{2,1,0:T(8,128)}), f32[16,64,512]{2,1,0:T(8,128)}, u32[]{:S(2)}, u32[]{:S(2)}) async-start(f32[16,64,512]{2,1,0:T(8,128)} %get-tuple-element.38), calls=%async_computation | async-start | bytes 4194304 | tf_op jit(solution)/shard_map/all_to_all | solution.py:229
  28.1 2.0 collective-permute-start
  31.7 32.5 %collective-permute-done = f32[4,64,512]{2,1,0:T(8,128)S(1)} collective-permute-done((f32[4,64,512]{2,1,0:T(8,128)S(1)}, f32[4,64,512]{2,1,0:T(8,128)S(1)}, u32[]{:S(2)}, u32[]{:S(2)}) %collective-permute-start) | collective-permute-done | bytes 524320 | tf_op jit(solution)/shard_map/near_freq_1/ppermute | solution.py:218
  66.5 10.0 %collective-permute-done.8.refs_3_ = f32[4,64,512]{2,1,0:T(8,128)S(1)} collective-permute-done((f32[4,64,512]{2,1,0:T(8,128)S(1)}, f32[4,64,512]{2,1,0:T(8,128)S(1)}, u32[]{:S(2)}, u32[]{:S(2)}) %collective-permute-start.8) | collective-permute-done | bytes 524320 | tf_op jit(solution)/shard_map/near_src_1/ppermute | solution.py:218
  79.2 2.7 %collective-permute-start.4 = (f32[2,64,512]{2,1,0:T(8,128)}, f32[2,64,512]{2,1,0:T(8,128)}, u32[]{:S(2)}, u32[]{:S(2)}) collective-permute-start(f32[2,64,512]{2,1,0:T(8,128)} %copy-done.1), channel_id=1, source_target_pairs={{0,20},{4,16},{8,28},{12,24},{16,4},{20,0},{24,12},{28,8},{1,21},{... | collective-permute-start | bytes 786440 | tf_op jit(solution)/shard_map/far_freq_1_1/ppermute | solution.py:218
  83.9 14.4 %collective-permute-done.3 = f32[2,64,512]{2,1,0:T(8,128)} collective-permute-done((f32[2,64,512]{2,1,0:T(8,128)}, f32[2,64,512]{2,1,0:T(8,128)}, u32[]{:S(2)}, u32[]{:S(2)}) %collective-permute-start.3) | collective-permute-done | bytes 262176 | tf_op jit(solution)/shard_map/far_freq_1_0/ppermute | solution.py:218
  99.0 5.0 %collective-permute-done.4 = f32[2,64,512]{2,1,0:T(8,128)} collective-permute-done((f32[2,64,512]{2,1,0:T(8,128)}, f32[2,64,512]{2,1,0:T(8,128)}, u32[]{:S(2)}, u32[]{:S(2)}) %collective-permute-start.4) | collective-permute-done | bytes 262176 | tf_op jit(solution)/shard_map/far_freq_1_1/ppermute | solution.py:218
  105.4 20.5 %collective-permute-done.5 = f32[2,64,512]{2,1,0:T(8,128)S(1)} collective-permute-done((f32[2,64,512]{2,1,0:T(8,128)S(1)}, f32[2,64,512]{2,1,0:T(8,128)S(1)}, u32[]{:S(2)}, u32[]{:S(2)}) %collective-permute-start.5) | collective-permute-done | bytes 262176 | tf_op jit(solution)/shard_map/far_freq_1_2/ppermute | solution.py:218
  128.6 1.9 slice_dynamic-update-slice_fusion.2
  133.6 5.4 %collective-permute-start.11 = (f32[2,64,512]{2,1,0:T(8,128)S(1)}, f32[2,64,512]{2,1,0:T(8,128)S(1)}, u32[]{:S(2)}, u32[]{:S(2)}) collective-permute-start(f32[2,64,512]{2,1,0:T(8,128)S(1)} %get-tuple-element.54), channel_id=1, source_target_pairs={{0,20},{4,16},{8,28},{12,24},{16,4},{20,0},{24,12},{28,8},{1,21},{... | collective-permute-start | bytes 786440 | tf_op jit(solution)/shard_map/far_freq_2_1/ppermute | solution.py:218
  139.8 1.7 constant_dynamic-update-slice_fusion.7
  141.4 3.7 %collective-permute-done.12.refs_4_ = f32[4,64,512]{2,1,0:T(8,128)S(1)} collective-permute-done((f32[4,64,512]{2,1,0:T(8,128)S(1)}, f32[4,64,512]{2,1,0:T(8,128)S(1)}, u32[]{:S(2)}, u32[]{:S(2)}) %collective-permute-start.12) | collective-permute-done | bytes 524320 | tf_op jit(solution)/shard_map/near_src_2/ppermute | solution.py:218
  145.7 1.7 constant_dynamic-update-slice_fusion.6
  147.3 6.9 %collective-permute-done.10 = f32[2,64,512]{2,1,0:T(8,128)S(1)} collective-permute-done((f32[2,64,512]{2,1,0:T(8,128)S(1)}, f32[2,64,512]{2,1,0:T(8,128)S(1)}, u32[]{:S(2)}, u32[]{:S(2)}) %collective-permute-start.10) | collective-permute-done | bytes 262176 | tf_op jit(solution)/shard_map/far_freq_2_0/ppermute | solution.py:218
  156.9 2.7 %collective-permute-done.11 = f32[2,64,512]{2,1,0:T(8,128)S(1)} collective-permute-done((f32[2,64,512]{2,1,0:T(8,128)S(1)}, f32[2,64,512]{2,1,0:T(8,128)S(1)}, u32[]{:S(2)}, u32[]{:S(2)}) %collective-permute-start.11) | collective-permute-done | bytes 262176 | tf_op jit(solution)/shard_map/far_freq_2_1/ppermute | solution.py:218
  161.1 1.7 constant_dynamic-update-slice_fusion.4.refs_0_
  163.5 2.7 %collective-permute-start.13 = (f32[2,64,512]{2,1,0:T(8,128)S(1)}, f32[2,64,512]{2,1,0:T(8,128)}, u32[]{:S(2)}, u32[]{:S(2)}) collective-permute-start(f32[2,64,512]{2,1,0:T(8,128)S(1)} %get-tuple-element.56), channel_id=1, source_target_pairs={{0,24},{4,28},{8,16},{12,20},{16,8},{20,12},{24,0},{28,4},{1,25},{... | collective-permute-start | bytes 786440 | tf_op jit(solution)/shard_map/far_freq_2_2/ppermute | solution.py:218
  166.9 11.9 %shard_map.128 = (f32[2,3,512,512]{3,2,1,0:T(8,128)}, f32[2,64,512]{2,1,0:T(8,128)}) custom-call(s32[3]{0:T(128)} %pad_add_fusion.place_ref, f32[16,64,512]{2,1,0:T(8,128)} %all-to-all-done.refs_0_, f32[16,64,512]{2,1,0:T(8,128)} %copy-done.3, f32[16,64,512]{2,1,0:T(8,128)} %collective-permute-done.9.refs_2_, ...), custom_call_target="tpu_custom_call", output_to_operand_aliasing={{1}: (4, {})} | custom-call | flops 1 | bytes 1 | tf_op jit(solution)/shard_map/pallas_call | solution.py:168
  180.9 3.1 %collective-permute-start.20 = (f32[2,64,512]{2,1,0:T(8,128)}, f32[2,64,512]{2,1,0:T(8,128)S(1)}, u32[]{:S(2)}, u32[]{:S(2)}) collective-permute-start(f32[2,64,512]{2,1,0:T(8,128)} %get-tuple-element.62), channel_id=1, source_target_pairs={{0,28},{4,24},{8,20},{12,16},{16,12},{20,8},{24,4},{28,0},{1,29},{... | collective-permute-start | bytes 786440 | tf_op jit(solution)/shard_map/far_freq_2_3/ppermute | solution.py:218
  185.5 1.7 constant_dynamic-update-slice_fusion.1
  187.2 4.5 %collective-permute-done.20 = f32[2,64,512]{2,1,0:T(8,128)S(1)} collective-permute-done((f32[2,64,512]{2,1,0:T(8,128)}, f32[2,64,512]{2,1,0:T(8,128)S(1)}, u32[]{:S(2)}, u32[]{:S(2)}) %collective-permute-start.20) | collective-permute-done | bytes 262176 | tf_op jit(solution)/shard_map/far_freq_2_3/ppermute | solution.py:218
  194.9 12.0 %shard_map.129.refs_10_ = f32[2,3,512,512]{3,2,1,0:T(8,128)} custom-call(s32[3]{0:T(128)} %pad_add_fusion.place_ref, f32[16,64,512]{2,1,0:T(8,128)} %constant_dynamic-update-slice_fusion.4.refs_0_, f32[16,64,512]{2,1,0:T(8,128)} %collective-permute-done.26.refs_1_, f32[4,64,512]{2,1,0:T(8,128)} %copy-done.9, ...), custom_call_target="tpu_custom_call", output_to_operand_aliasing={{}: (11, {})} | custom-call | flops 6442450944 | bytes 10485760 | tf_op jit(solution)/shard_map/pallas_call | solution.py:168
  208.1 11.8 %shard_map.130 = f32[2,3,512,512]{3,2,1,0:T(8,128)} custom-call(s32[3]{0:T(128)} %pad_add_fusion.place_ref, f32[16,64,512]{2,1,0:T(8,128)} %constant_dynamic-update-slice_fusion.refs_0_, f32[16,64,512]{2,1,0:T(8,128)} %collective-permute-done.23.refs_1_, f32[4,64,512]{2,1,0:T(8,128)} %copy-done.9, ...), custom_call_target="tpu_custom_call", output_to_operand_aliasing={{}: (11, {})} | custom-call | flops 6442450944 | bytes 10485760 | tf_op jit(solution)/shard_map/pallas_call | solution.py:168
  (92 shorter events, 34.2 us)
Async XLA Ops:
  20.9 55.7 %all-to-all-start = ((f32[16,64,512]{2,1,0:T(8,128)}), f32[16,64,512]{2,1,0:T(8,128)}, u32[]{:S(2)}, u32[]{:S(2)}) async-start(f32[16,64,512]{2,1,0:T(8,128)} %get-tuple-element.38), calls=%async_computation | async-start | bytes 4194304 | tf_op jit(solution)/shard_map/all_to_all | solution.py:229
  28.1 36.1 %collective-permute-start = (f32[4,64,512]{2,1,0:T(8,128)S(1)}, f32[4,64,512]{2,1,0:T(8,128)S(1)}, u32[]{:S(2)}, u32[]{:S(2)}) collective-permute-start(f32[4,64,512]{2,1,0:T(8,128)S(1)} %get-tuple-element.36), channel_id=1, source_target_pairs={{0,4},{4,0},{8,12},{12,8},{16,20},{20,16},{24,28},{28,24},{1,5},{5... | collective-permute-start | bytes 1572872 | tf_op jit(solution)/shard_map/near_freq_1/ppermute | solution.py:218
  30.2 35.6 %collective-permute-start.7 = (f32[4,64,512]{2,1,0:T(8,128)S(1)}, f32[4,64,512]{2,1,0:T(8,128)S(1)}, u32[]{:S(2)}, u32[]{:S(2)}) collective-permute-start(f32[4,64,512]{2,1,0:T(8,128)S(1)} %get-tuple-element.35), channel_id=1, source_target_pairs={{0,2},{2,0},{1,3},{3,1},{4,6},{6,4},{5,7},{7,5},{8,10},{10,8},{9,1... | collective-permute-start | bytes 1572872 | tf_op jit(solution)/shard_map/near_src_0/ppermute | solution.py:218
  76.6 51.0 %collective-permute-start.9 = (f32[16,64,512]{2,1,0:T(8,128)}, f32[16,64,512]{2,1,0:T(8,128)}, u32[]{:S(2)}, u32[]{:S(2)}) collective-permute-start(f32[16,64,512]{2,1,0:T(8,128)} %all-to-all-done.refs_0_), channel_id=1, source_target_pairs={{0,2},{2,0},{1,3},{3,1},{4,6},{6,4},{5,7},{7,5},{8,10},{10,8},{9,1... | collective-permute-start | bytes 6291464 | tf_op jit(solution)/shard_map/first_src/ppermute | solution.py:218
  78.1 20.2 %collective-permute-start.3 = (f32[2,64,512]{2,1,0:T(8,128)}, f32[2,64,512]{2,1,0:T(8,128)}, u32[]{:S(2)}, u32[]{:S(2)}) collective-permute-start(f32[2,64,512]{2,1,0:T(8,128)} %copy-done.2), channel_id=1, source_target_pairs={{0,16},{4,20},{8,24},{12,28},{16,0},{20,4},{24,8},{28,12},{1,17},{... | collective-permute-start | bytes 786440 | tf_op jit(solution)/shard_map/far_freq_1_0/ppermute | solution.py:218
  79.2 24.9 %collective-permute-start.4 = (f32[2,64,512]{2,1,0:T(8,128)}, f32[2,64,512]{2,1,0:T(8,128)}, u32[]{:S(2)}, u32[]{:S(2)}) collective-permute-start(f32[2,64,512]{2,1,0:T(8,128)} %copy-done.1), channel_id=1, source_target_pairs={{0,20},{4,16},{8,28},{12,24},{16,4},{20,0},{24,12},{28,8},{1,21},{... | collective-permute-start | bytes 786440 | tf_op jit(solution)/shard_map/far_freq_1_1/ppermute | solution.py:218
  81.8 45.7 %collective-permute-start.1 = (f32[4,64,512]{2,1,0:T(8,128)S(1)}, f32[4,64,512]{2,1,0:T(8,128)S(1)}, u32[]{:S(2)}, u32[]{:S(2)}) collective-permute-start(f32[4,64,512]{2,1,0:T(8,128)S(1)} %get-tuple-element.39), channel_id=1, source_target_pairs={{0,8},{4,12},{8,0},{12,4},{16,24},{20,28},{24,16},{28,20},{1,9},{5... | collective-permute-start | bytes 1572872 | tf_op jit(solution)/shard_map/near_freq_2/ppermute | solution.py:218
  83.1 44.5 %collective-permute-start.2 = (f32[4,64,512]{2,1,0:T(8,128)S(1)}, f32[4,64,512]{2,1,0:T(8,128)S(1)}, u32[]{:S(2)}, u32[]{:S(2)}) collective-permute-start(f32[4,64,512]{2,1,0:T(8,128)S(1)} %get-tuple-element.41), channel_id=1, source_target_pairs={{0,12},{4,8},{8,4},{12,0},{16,28},{20,24},{24,20},{28,16},{1,13},{... | collective-permute-start | bytes 1572872 | tf_op jit(solution)/shard_map/near_freq_3/ppermute | solution.py:218
  98.3 27.6 %collective-permute-start.5 = (f32[2,64,512]{2,1,0:T(8,128)S(1)}, f32[2,64,512]{2,1,0:T(8,128)S(1)}, u32[]{:S(2)}, u32[]{:S(2)}) collective-permute-start(f32[2,64,512]{2,1,0:T(8,128)S(1)} %get-tuple-element.48), channel_id=1, source_target_pairs={{0,24},{4,28},{8,16},{12,20},{16,8},{20,12},{24,0},{28,4},{1,25},{... | collective-permute-start | bytes 786440 | tf_op jit(solution)/shard_map/far_freq_1_2/ppermute | solution.py:218
  104.0 23.6 %collective-permute-start.6 = (f32[2,64,512]{2,1,0:T(8,128)S(1)}, f32[2,64,512]{2,1,0:T(8,128)}, u32[]{:S(2)}, u32[]{:S(2)}) collective-permute-start(f32[2,64,512]{2,1,0:T(8,128)S(1)} %get-tuple-element.50), channel_id=1, source_target_pairs={{0,28},{4,24},{8,20},{12,16},{16,12},{20,8},{24,4},{28,0},{1,29},{... | collective-permute-start | bytes 786440 | tf_op jit(solution)/shard_map/far_freq_1_3/ppermute | solution.py:218
  127.6 35.9 %collective-permute-start.14 = (f32[16,64,512]{2,1,0:T(8,128)}, f32[16,64,512]{2,1,0:T(8,128)S(1)}, u32[]{:S(2)}, u32[]{:S(2)}) collective-permute-start(f32[16,64,512]{2,1,0:T(8,128)} %all-to-all-done.refs_0_), channel_id=1, source_target_pairs={{0,1},{1,0},{2,3},{3,2},{4,5},{5,4},{6,7},{7,6},{8,9},{9,8},{10,11... | collective-permute-start | bytes 6291464 | tf_op jit(solution)/shard_map/first_rcv/ppermute | solution.py:218
  130.4 14.7 %collective-permute-start.12 = (f32[4,64,512]{2,1,0:T(8,128)S(1)}, f32[4,64,512]{2,1,0:T(8,128)S(1)}, u32[]{:S(2)}, u32[]{:S(2)}) collective-permute-start(f32[4,64,512]{2,1,0:T(8,128)S(1)} %collective-permute-done.1), channel_id=1, source_target_pairs={{0,2},{2,0},{1,3},{3,1},{4,6},{6,4},{5,7},{7,5},{8,10},{10,8},{9,1... | collective-permute-start | bytes 1572872 | tf_op jit(solution)/shard_map/near_src_2/ppermute | solution.py:218
  131.0 25.4 %collective-permute-start.15 = (f32[4,64,512]{2,1,0:T(8,128)S(1)}, f32[4,64,512]{2,1,0:T(8,128)S(1)}, u32[]{:S(2)}, u32[]{:S(2)}) collective-permute-start(f32[4,64,512]{2,1,0:T(8,128)S(1)} %collective-permute-done.2), channel_id=1, source_target_pairs={{0,2},{2,0},{1,3},{3,1},{4,6},{6,4},{5,7},{7,5},{8,10},{10,8},{9,1... | collective-permute-start | bytes 1572872 | tf_op jit(solution)/shard_map/near_src_3/ppermute | solution.py:218
  133.3 21.0 %collective-permute-start.10 = (f32[2,64,512]{2,1,0:T(8,128)S(1)}, f32[2,64,512]{2,1,0:T(8,128)S(1)}, u32[]{:S(2)}, u32[]{:S(2)}) collective-permute-start(f32[2,64,512]{2,1,0:T(8,128)S(1)} %get-tuple-element.52), channel_id=1, source_target_pairs={{0,16},{4,20},{8,24},{12,28},{16,0},{20,4},{24,8},{28,12},{1,17},{... | collective-permute-start | bytes 786440 | tf_op jit(solution)/shard_map/far_freq_2_0/ppermute | solution.py:218
  133.6 26.1 %collective-permute-start.11 = (f32[2,64,512]{2,1,0:T(8,128)S(1)}, f32[2,64,512]{2,1,0:T(8,128)S(1)}, u32[]{:S(2)}, u32[]{:S(2)}) collective-permute-start(f32[2,64,512]{2,1,0:T(8,128)S(1)} %get-tuple-element.54), channel_id=1, source_target_pairs={{0,20},{4,16},{8,28},{12,24},{16,4},{20,0},{24,12},{28,8},{1,21},{... | collective-permute-start | bytes 786440 | tf_op jit(solution)/shard_map/far_freq_2_1/ppermute | solution.py:218
  145.2 17.6 %collective-permute-start.18 = (f32[2,64,512]{2,1,0:T(8,128)S(1)}, f32[2,64,512]{2,1,0:T(8,128)S(1)}, u32[]{:S(2)}, u32[]{:S(2)}) collective-permute-start(f32[2,64,512]{2,1,0:T(8,128)S(1)} %collective-permute-done.5), channel_id=1, source_target_pairs={{0,2},{2,0},{1,3},{3,1},{4,6},{6,4},{5,7},{7,5},{8,10},{10,8},{9,1... | collective-permute-start | bytes 786440 | tf_op jit(solution)/shard_map/far_src_1_2/ppermute | solution.py:218
  154.3 24.5 %collective-permute-start.19 = (f32[2,64,512]{2,1,0:T(8,128)}, f32[2,64,512]{2,1,0:T(8,128)}, u32[]{:S(2)}, u32[]{:S(2)}) collective-permute-start(f32[2,64,512]{2,1,0:T(8,128)} %collective-permute-done.6), channel_id=1, source_target_pairs={{0,2},{2,0},{1,3},{3,1},{4,6},{6,4},{5,7},{7,5},{8,10},{10,8},{9,1... | collective-permute-start | bytes 786440 | tf_op jit(solution)/shard_map/far_src_1_3/ppermute | solution.py:218
  156.4 23.8 %collective-permute-start.16 = (f32[2,64,512]{2,1,0:T(8,128)}, f32[2,64,512]{2,1,0:T(8,128)}, u32[]{:S(2)}, u32[]{:S(2)}) collective-permute-start(f32[2,64,512]{2,1,0:T(8,128)} %collective-permute-done.3), channel_id=1, source_target_pairs={{0,2},{2,0},{1,3},{3,1},{4,6},{6,4},{5,7},{7,5},{8,10},{10,8},{9,1... | collective-permute-start | bytes 786440 | tf_op jit(solution)/shard_map/far_src_1_0/ppermute | solution.py:218
  159.7 21.2 %collective-permute-start.17 = (f32[2,64,512]{2,1,0:T(8,128)}, f32[2,64,512]{2,1,0:T(8,128)}, u32[]{:S(2)}, u32[]{:S(2)}) collective-permute-start(f32[2,64,512]{2,1,0:T(8,128)} %collective-permute-done.4), channel_id=1, source_target_pairs={{0,2},{2,0},{1,3},{3,1},{4,6},{6,4},{5,7},{7,5},{8,10},{10,8},{9,1... | collective-permute-start | bytes 786440 | tf_op jit(solution)/shard_map/far_src_1_1/ppermute | solution.py:218
  163.5 31.4 %collective-permute-start.26 = (f32[16,64,512]{2,1,0:T(8,128)}, f32[16,64,512]{2,1,0:T(8,128)}, u32[]{:S(2)}, u32[]{:S(2)}) collective-permute-start(f32[16,64,512]{2,1,0:T(8,128)} %constant_dynamic-update-slice_fusion.4.refs_0_), channel_id=1, source_target_pairs={{0,1},{1,0},{2,3},{3,2},{4,5},{5,4},{6,7},{7,6},{8,9},{9,8},{10,11... | collective-permute-start | bytes 6291464 | tf_op jit(solution)/shard_map/rcv_1/ppermute | solution.py:218
  163.5 22.0 %collective-permute-start.13 = (f32[2,64,512]{2,1,0:T(8,128)S(1)}, f32[2,64,512]{2,1,0:T(8,128)}, u32[]{:S(2)}, u32[]{:S(2)}) collective-permute-start(f32[2,64,512]{2,1,0:T(8,128)S(1)} %get-tuple-element.56), channel_id=1, source_target_pairs={{0,24},{4,28},{8,16},{12,20},{16,8},{20,12},{24,0},{28,4},{1,25},{... | collective-permute-start | bytes 786440 | tf_op jit(solution)/shard_map/far_freq_2_2/ppermute | solution.py:218
  178.8 13.7 %collective-permute-start.21 = (f32[2,64,512]{2,1,0:T(8,128)S(1)}, f32[2,64,512]{2,1,0:T(8,128)S(1)}, u32[]{:S(2)}, u32[]{:S(2)}) collective-permute-start(f32[2,64,512]{2,1,0:T(8,128)S(1)} %copy-done.6), channel_id=1, source_target_pairs={{0,2},{2,0},{1,3},{3,1},{4,6},{6,4},{5,7},{7,5},{8,10},{10,8},{9,1... | collective-permute-start | bytes 786440 | tf_op jit(solution)/shard_map/far_src_2_0/ppermute | solution.py:218
  192.9 14.6 %collective-permute-start.23 = (f32[16,64,512]{2,1,0:T(8,128)}, f32[16,64,512]{2,1,0:T(8,128)}, u32[]{:S(2)}, u32[]{:S(2)}) collective-permute-start(f32[16,64,512]{2,1,0:T(8,128)} %constant_dynamic-update-slice_fusion.refs_0_), channel_id=1, source_target_pairs={{0,1},{1,0},{2,3},{3,2},{4,5},{5,4},{6,7},{7,6},{8,9},{9,8},{10,11... | collective-permute-start | bytes 6291464 | tf_op jit(solution)/shard_map/rcv_2/ppermute | solution.py:218
  192.9 14.0 %collective-permute-start.24 = (f32[2,64,512]{2,1,0:T(8,128)}, f32[2,64,512]{2,1,0:T(8,128)S(1)}, u32[]{:S(2)}, u32[]{:S(2)}) collective-permute-start(f32[2,64,512]{2,1,0:T(8,128)} %collective-permute-done.13), channel_id=1, source_target_pairs={{0,2},{2,0},{1,3},{3,1},{4,6},{6,4},{5,7},{7,5},{8,10},{10,8},{9,1... | collective-permute-start | bytes 786440 | tf_op jit(solution)/shard_map/far_src_2_2/ppermute | solution.py:218
  (22 other events, 193.8 us)
